TPU v7x, 32 devices: a whole 2x2x4 slice. The times are simulated.
32 devices in a mesh: shard: 8 (over z, x), rep: 4 (over y, core).
Axes of the slice: x: 2, y: 2, z: 4, core: 2. Of those that a mesh axis runs over, the one named last changes fastest.
Arguments:
- tokens: bfloat16 [8, 1024, 1024], P('rep', 'shard'), may hold values from -6 to 6
- lengths: int32 [8], P('rep'), may hold values from 512 to 1024, as said below
- expert_ids: int32 [8, 1024, 2], P('rep', 'shard'), may hold values from 0 to 3, all different within a row
- buckets: int32 [2047], replicated, may hold values from 0 to 31
- norm1_gain: bfloat16 [1024], P('shard'), may hold values from 0.5 to 1.5
- w_query: bfloat16 [1024, 1024], P('shard'), may hold values from -0.1875 to 0.1875
- w_key: bfloat16 [1024, 1024], P('shard'), may hold values from -0.1875 to 0.1875
- w_value: bfloat16 [1024, 1024], P('shard'), may hold values from -0.1875 to 0.1875
- w_out: bfloat16 [1024, 1024], P('shard'), may hold values from -0.75 to 0.75
- rel_bias: bfloat16 [32, 16], P(None, 'shard'), may hold values from -4 to 4
- norm2_gain: bfloat16 [1024], P('shard'), may hold values from 0.5 to 1.5
- w_router: bfloat16 [1024, 4], P('shard'), may hold values from -0.125 to 0.125
- w_gate: bfloat16 [4, 2816, 1024], P(None, 'shard'), may hold values from -0.1875 to 0.1875
- w_up: bfloat16 [4, 2816, 1024], P(None, 'shard'), may hold values from -0.1875 to 0.1875
- w_down: bfloat16 [4, 2816, 1024], P(None, 'shard'), may hold values from -0.109375 to 0.109375
- cotangent: bfloat16 [8, 1024, 1024], P('rep', 'shard'), may hold values from -6 to 6
Outputs:
- block_out: bfloat16 [8, 1024, 1024], P('rep', 'shard')
- grad_tokens: float32 [8, 1024, 1024], P('rep', 'shard')
- grad_norm1_gain: float32 [1024], P('shard')
- grad_w_query: float32 [1024, 1024], P('shard')
- grad_w_key: float32 [1024, 1024], P('shard')
- grad_w_value: float32 [1024, 1024], P('shard')
- grad_w_out: float32 [1024, 1024], P('shard')
- grad_rel_bias: float32 [32, 16], P(None, 'shard')
- grad_norm2_gain: float32 [1024], P('shard')
- grad_w_router: float32 [1024, 4], P('shard')
- grad_w_gate: float32 [4, 2816, 1024], P(None, 'shard')
- grad_w_up: float32 [4, 2816, 1024], P(None, 'shard')
- grad_w_down: float32 [4, 2816, 1024], P(None, 'shard')
Inputs may be any that keep to these rules, and one draw needn't show every extreme that they name: `lengths`: in every group of 2 consecutive sequences at least one has length 1024. `expert_ids`: the two experts of a position differ.
All inputs are finite; a program needn't handle non-finite values.
Results may differ from a plain program's by a relative error of at most 0.022.
Values may be sent and summed in bfloat16 or wider, within the bound.
No kernel may reach another device: no remote copies, remote signals or barrier semaphores. Data moves between devices by JAX's collectives and lax.ppermute only.
A program may use at most 320 MiB of HBM per device.

v0:
```python
import functools

import jax
import jax.numpy as jnp
from jax import lax
from jax.experimental import pallas as pl
from jax.experimental.pallas import tpu as pltpu
from jax.sharding import PartitionSpec as P

epsilon = 1e-06
highest = lax.Precision.HIGHEST
bf16 = jnp.bfloat16
f32 = jnp.float32
vmem_limit = 58 * 1024 * 1024
whole_ref = pl.BlockSpec(memory_space=pltpu.VMEM)


def dot_nt(left, right):
    return lax.dot_general(left, right, (((1,), (1,)), ((), ())), preferred_element_type=f32)


def dot_tn(left, right):
    return lax.dot_general(left, right, (((0,), (0,)), ((), ())), preferred_element_type=f32)


def dot_nn(left, right):
    return lax.dot_general(left, right, (((1,), (0,)), ((), ())), preferred_element_type=f32)


def ring_index(place, count):
    return jnp.where(place < count // 2, 2 * place, 2 * count - 1 - 2 * place)


def ring_place(index, count):
    return jnp.where(index % 2 == 0, index // 2, count - 1 - index // 2)


def ring_send(value, step, count):
    order = [2 * i if i < count // 2 else 2 * count - 1 - 2 * i for i in range(count)]
    pairs = [(order[i], order[(i + step) % count]) for i in range(count)]
    return lax.ppermute(value, "shard", pairs)


def after(value, *waits):
    if not jax.tree.leaves(waits):
        return value
    flat, tree = jax.tree.flatten(value)
    held = lax.optimization_barrier(tuple(flat) + tuple(jax.tree.leaves(waits)))
    return tree.unflatten(held[: len(flat)])


def halve(value):
    half = value.shape[0] // 2
    return value[:half], value[half:]


class Gather:
    def __init__(self, value, count, split=None):
        self.count, self.step, self.split = count, 1, split or halve
        self.ahead = self.behind = value
        self.pieces = [(0, None, value)]
        self.done = False

    def hop(self, *waits):
        behind, ahead = after((self.behind, self.ahead), *waits)
        far = self.count // 2
        if self.step < far:
            self.behind = ring_send(behind, 1, self.count)
            self.ahead = ring_send(ahead, -1, self.count)
            self.pieces += [(self.count - self.step, None, self.behind), (self.step, None, self.ahead)]
            self.step += 1
        else:
            self.behind = ring_send(self.split(behind)[0], 1, self.count)
            self.ahead = ring_send(self.split(ahead)[1], -1, self.count)
            self.pieces += [(far, 0, self.behind), (far, 1, self.ahead)]
            self.done = True

    def last(self):
        return (self.behind, self.ahead)


def add_low(left, right):
    return (left.astype(f32) + right.astype(f32)).astype(bf16)


def ring_add_kernel(half, firsts, right, left, *refs):
    count = len(firsts)
    owns = (refs[:count], refs[count : 2 * count])
    outs = refs[2 * count :]
    total = outs[0].shape[0]
    for come, own, out, begin in zip((right, left), owns, outs, (0, total - half)):
        for source, first in zip(own, firsts):
            last = first + source.shape[1]
            low, high = max(first, begin), min(last, begin + half)
            if low < high:
                summed = source[0, low - first : high - first, :].astype(f32)
                summed = summed + come[low - begin : high - begin, :].astype(f32)
                out[low:high, :] = summed.astype(bf16)
            if first < min(low, last):
                out[first : min(low, last), :] = source[0, : min(low, last) - first, :]
            if max(high, first) < last:
                out[max(high, first) : last, :] = source[0, max(high, first) - first :, :]


def ring_add(right, left, own_right, own_left, rows):
    width = right.shape[1]
    total = sum(rows)
    firsts = [sum(rows[:i]) for i in range(len(rows))]
    full = lambda *shape: pl.BlockSpec(shape, lambda i: (0,) * len(shape))
    part = lambda spot, count: pl.BlockSpec((1, count, width), lambda i: (spot[1], spot[2], 0))
    shape = jax.ShapeDtypeStruct((total, width), bf16)
    return pl.pallas_call(
        functools.partial(ring_add_kernel, right.shape[0], firsts),
        out_shape=(shape, shape),
        grid=(1,),
        in_specs=[full(*right.shape)] * 2
        + [part(spot, count) for spot, count in zip(own_right, rows)]
        + [part(spot, count) for spot, count in zip(own_left, rows)],
        out_specs=(full(total, width),) * 2,
        compiler_params=pltpu.CompilerParams(vmem_limit_bytes=14 * 2**20),
        cost_estimate=pl.CostEstimate(
            flops=2 * total * width, bytes_accessed=1000, transcendentals=0
        ),
        name="ring_add",
    )(right, left, *[spot[0] for spot in own_right], *[spot[0] for spot in own_left])


class Sum:
    def __init__(self, sources, count):
        self.sources, self.count, self.step = sources, count, count // 2
        self.rows = [rows for array, block, rows in sources]
        self.right = self.left = None
        self.done = False

    def chunk(self, distance):
        return jnp.concatenate(
            [array[distance, block * rows : (block + 1) * rows] for array, block, rows in self.sources],
            axis=0,
        )

    def hop(self, *waits):
        if self.right is None:
            right, left = halve(self.chunk(self.step))
        else:
            spots = [
                [(array, distance, block) for array, block, rows in self.sources]
                for distance in (self.step, self.count - self.step)
            ]
            right, left = ring_add(self.right, self.left, *spots, self.rows)
        right, left = after((right, left), *waits)
        self.right = ring_send(right, 1, self.count)
        self.left = ring_send(left, -1, self.count)
        self.step -= 1
        self.done = self.step == 0

    def last(self):
        return (self.right, self.left)

    def total(self):
        total = self.chunk(0).astype(f32)
        return total + self.right.astype(f32) + self.left.astype(f32)


def fire(rings, *waits):
    rings = [ring for ring in rings if not ring.done]
    waits = waits + tuple(ring.last() for ring in rings if ring.last()[0] is not None)
    for ring in rings:
        ring.hop(*waits)


def lasts(rings):
    return tuple(ring.last() for ring in rings)


def swap(value, axis, count, bit):
    return lax.ppermute(value, axis, [(i, i ^ bit) for i in range(count)])


def bits_of(count):
    return [1 << i for i in range(count.bit_length() - 1)]


def rep_scatter(value, count, me, *waits):
    for bit in bits_of(count):
        value = value.reshape((value.shape[0] // 2, 2) + value.shape[1:])
        side = (me // bit) % 2
        sent = lax.dynamic_index_in_dim(value, 1 - side, 1, keepdims=False)
        kept = lax.dynamic_index_in_dim(value, side, 1, keepdims=False)
        if bit > 1:
            sent = after(sent, *waits)
        value = add_low(kept, swap(sent, "rep", count, bit))
    return value[0]


def rep_parts(value, count, me):
    parts, tags = [value], [0]
    for bit in bits_of(count)[::-1]:
        parts = parts + [swap(part, "rep", count, bit) for part in parts]
        tags = tags + [tag ^ bit for tag in tags]
    return parts, (me ^ jnp.array(tags, jnp.int32))


def rep_order(count):
    tags = [0]
    for bit in bits_of(count)[::-1]:
        tags = tags + [tag ^ bit for tag in tags]
    return [tags.index(tag) for tag in range(count)]


def weave_kernel(count, spots, *refs):
    parts, out, sems = refs[:count], refs[count], refs[count + 1]
    copies = [
        pltpu.make_async_copy(part, out.at[:, spots[i]], sems.at[i])
        for i, part in enumerate(parts)
    ]
    for copy in copies:
        copy.start()
    for copy in copies:
        copy.wait()


def weave(parts, spots):
    first, rows, columns = parts[0].shape
    anywhere = pl.BlockSpec(memory_space=pl.ANY)
    out = pl.pallas_call(
        functools.partial(weave_kernel, len(parts)),
        out_shape=jax.ShapeDtypeStruct((first, len(parts), rows, columns), parts[0].dtype),
        in_specs=[pl.BlockSpec(memory_space=pltpu.SMEM)] + [anywhere] * len(parts),
        out_specs=anywhere,
        scratch_shapes=[pltpu.SemaphoreType.DMA((len(parts),))],
        compiler_params=pltpu.CompilerParams(vmem_limit_bytes=2**20),
        name="weave",
    )(spots, *parts)
    return out.reshape(first * len(parts) * rows, columns)


def widen_kernel(parts, meta, kept, got, kept_other, got_other, out, *scratch):
    held, wide, in_sems, out_sems = scratch
    half = kept.shape[0]
    rows = half // parts
    sources = (kept, got, kept_other, got_other)
    ins = [
        [
            pltpu.make_async_copy(
                source.at[pl.ds(part * rows, rows), :],
                held.at[number, pl.ds(part * rows, rows), :],
                in_sems.at[number * parts + part],
            )
            for number, source in enumerate(sources)
        ]
        for part in range(parts)
    ]
    for part in range(parts):
        for copy in ins[part]:
            copy.start()
    outs = []
    for part in range(parts):
        for copy in ins[part]:
            copy.wait()
        at = slice(part * rows, (part + 1) * rows)
        for pair in range(2):
            total = held[2 * pair, at, :].astype(f32) + held[2 * pair + 1, at, :].astype(f32)
            wide[pair, at, :] = total
            side = meta[0] if pair == 0 else 1 - meta[0]
            start = pl.multiple_of(side * half + part * rows, 8)
            outs.append(
                pltpu.make_async_copy(
                    wide.at[pair, pl.ds(part * rows, rows), :],
                    out.at[pl.ds(start, rows), :],
                    out_sems.at[pair * parts + part],
                )
            )
            outs[-1].start()
    for copy in outs:
        copy.wait()


def widen(side, kept, got, kept_other, got_other):
    half, width = kept.shape
    parts = 4 if half % 64 == 0 else 2 if half % 32 == 0 else 1
    anywhere = pl.BlockSpec(memory_space=pl.ANY)
    return pl.pallas_call(
        functools.partial(widen_kernel, parts),
        out_shape=jax.ShapeDtypeStruct((2 * half, width), f32),
        in_specs=[pl.BlockSpec(memory_space=pltpu.SMEM)] + [anywhere] * 4,
        out_specs=anywhere,
        scratch_shapes=[
            pltpu.VMEM((4, half, width), bf16),
            pltpu.VMEM((2, half, width), f32),
            pltpu.SemaphoreType.DMA((4 * parts,)),
            pltpu.SemaphoreType.DMA((2 * parts,)),
        ],
        compiler_params=pltpu.CompilerParams(vmem_limit_bytes=16 * 2**20),
        name="widen",
    )(side, kept, got, kept_other, got_other)


class RepTotal:
    def __init__(self, value, count, me):
        self.count, self.side = count, me % 2
        value = value.reshape((2, value.shape[0] // 2) + value.shape[1:])
        sent = lax.dynamic_index_in_dim(value, 1 - self.side, 0, keepdims=False)
        self.kept = lax.dynamic_index_in_dim(value, self.side, 0, keepdims=False)
        self.got = swap(sent, "rep", count, 1)

    def cross(self, *waits):
        kept = add_low(self.kept, self.got)
        for bit in bits_of(self.count)[1:-1]:
            kept = add_low(kept, swap(kept, "rep", self.count, bit))
        self.kept = after(kept, *waits)
        self.got = swap(self.kept, "rep", self.count, self.count // 2)
        self.kept_other = swap(self.kept, "rep", self.count, 1)

    def finish(self):
        got_other = swap(self.got, "rep", self.count, 1)
        side = self.side.reshape(1).astype(jnp.int32)
        return widen(side, self.kept, self.got, self.kept_other, got_other)


def bias_kernel(vec, table, turned):
    heads, _, width = table.shape
    for head in range(heads):
        line = jnp.broadcast_to(vec[head : head + 1, :], (128, vec.shape[1]))
        line = pltpu.roll(line, vec.shape[1] - 127, 1, stride=1, stride_axis=0)
        table[head] = line[:, :width]
        for first in range(0, width, 128):
            turned[head, first : first + 128, :] = line[:, first : first + 128].T


def bias_tables(vec):
    heads, length = vec.shape
    width = length - 128
    return pl.pallas_call(
        bias_kernel,
        out_shape=(
            jax.ShapeDtypeStruct((heads, 128, width), f32),
            jax.ShapeDtypeStruct((heads, width, 128), f32),
        ),
        in_specs=[whole_ref],
        out_specs=[whole_ref] * 2,
        compiler_params=pltpu.CompilerParams(vmem_limit_bytes=24 * 2**20),
        name="bias_tables",
    )(vec)


def attend_kernel(seq, seqs, places, heads, head_size, riders, meta, *refs):
    pieces = refs[: len(places)]
    cotangent, weight, bias, tokens_out, qkv_out, mixed_out, *more = refs[len(places) :]
    sems = more[-1]
    length = meta[seq]
    span = cotangent.shape[0]
    seq_len = tokens_out.shape[0]
    each = heads * head_size
    blocks = seq_len // 128
    copies = []
    for number, ((distance, first), piece) in enumerate(zip(places, pieces)):
        start = pl.multiple_of(meta[seqs + distance] * span, 16)
        copies.append(
            pltpu.make_async_copy(
                piece.at[pl.ds(first, span), :],
                tokens_out.at[pl.ds(start, span), :],
                sems.at[number],
            )
        )
        copies[-1].start()
    for number, (distance, first) in enumerate(riders):
        copies.append(
            pltpu.make_async_copy(
                pieces[number].at[pl.ds(first, more[0].shape[1]), :],
                more[0].at[distance],
                sems.at[len(places) + number],
            )
        )
        copies[-1].start()
    mixed_out[0:span, :] = cotangent[...]
    for copy in copies:
        copy.wait()
    for first in range(0, seq_len, 256):
        rows = slice(first, first + 256)
        low = tokens_out[rows, :]
        wide = low.astype(f32)
        factor = lax.rsqrt(jnp.mean(wide * wide, axis=-1, keepdims=True) + epsilon)
        made = dot_nn(low, weight[...]) * factor
        for part in range(3 * heads):
            cut = made[:, part * head_size : (part + 1) * head_size]
            if part < heads:
                cut = cut.astype(bf16).astype(f32) * head_size ** (-0.5)
            qkv_out[part, rows, :] = cut.astype(bf16)
    for head in range(heads):
        keys = qkv_out[heads + head]
        values = qkv_out[2 * heads + head]
        for block in range(0, blocks, 2):
            queries = qkv_out[head, block * 128 : block * 128 + 256, :]
            scores = dot_nt(queries, keys)
            first_col = (blocks - 1 - block) * 128
            added = jnp.concatenate(
                [
                    bias[head, :, first_col : first_col + seq_len],
                    bias[head, :, first_col - 128 : first_col - 128 + seq_len],
                ],
                axis=0,
            )
            column = lax.broadcasted_iota(jnp.int32, scores.shape, 1)
            scores = jnp.where(column < length, scores + added, -1e30)
            top = jnp.max(scores, axis=-1, keepdims=True)
            weights = jnp.exp(scores - top)
            total = jnp.sum(weights, axis=-1, keepdims=True)
            mixed = dot_nn(weights.astype(bf16), values) / total
            mixed = mixed.astype(bf16)
            for part in range(256 // span):
                lane = (block * 128 // span + part) * each + head * head_size
                mixed_out[span : 2 * span, lane : lane + head_size] = mixed[
                    part * span : (part + 1) * span, :
                ]


def attend(meta, seq, seqs, pieces, cotangent, weight, bias, heads, head_size):
    width = weight.shape[0]
    span = cotangent.shape[0]
    pieces = [(d, half, piece) for d, half, piece in pieces if half is None or half == seq]
    places = [(d, seq * span if half is None else 0) for d, half, piece in pieces]
    seq_len = span * len(pieces)
    full = lambda *shape: pl.BlockSpec(shape, lambda i, meta: (0,) * len(shape))
    shapes = [(seq_len, width), (3 * heads, seq_len, head_size), (2 * span, width)]
    riders = []
    if seq == 0:
        extra = pieces[0][2].shape[0] - seqs * span
        riders = [(d, seqs * span if half is None else span) for d, half, piece in pieces]
        shapes.append((len(pieces), extra, width))
    return pl.pallas_call(
        functools.partial(attend_kernel, seq, seqs, places, heads, head_size, riders),
        out_shape=tuple(jax.ShapeDtypeStruct(shape, bf16) for shape in shapes),
        grid_spec=pltpu.PrefetchScalarGridSpec(
            num_scalar_prefetch=1,
            grid=(1,),
            in_specs=[pl.BlockSpec(memory_space=pl.ANY)] * len(pieces)
            + [full(*cotangent.shape), full(*weight.shape), full(*bias.shape)],
            out_specs=[full(*shape) for shape in shapes],
            scratch_shapes=[pltpu.SemaphoreType.DMA((2 * len(pieces),))],
        ),
        compiler_params=pltpu.CompilerParams(vmem_limit_bytes=28 * 2**20),
        cost_estimate=pl.CostEstimate(
            flops=8 * 10**9, bytes_accessed=1000, transcendentals=heads * seq_len * seq_len
        ),
        name="attend",
    )(meta, *[piece for d, half, piece in pieces], cotangent, weight, bias)


def experts_kernel(static, meta, *refs):
    count, span, seqs, expert_count, capacity, seq, blocks, kinds, alias_count = static
    tokens_hbm, *pieces = refs[: 1 + len(kinds)]
    refs = refs[1 + len(kinds) :]
    gain, router_weight, ids, gain_in, out_weight, gate_weight, up_weight, down_weight = refs[:8]
    refs = refs[8 + alias_count :]
    buffers, sums_out, gain_out, refs = refs[:8], refs[8], refs[9], refs[10:]
    staged, refs = refs[:8], refs[8:]
    heads_all, mix_all, tokens_all, context_all, sems_all, in_sems_all = refs
    _, rows, width = tokens_all.shape
    each = width // count
    seq_len = span * count
    members = rows // span
    length, me = meta[seq], meta[meta.shape[0] - 1]


    def bring(number_of_block, block):
        tokens, context = tokens_all.at[number_of_block], context_all.at[number_of_block]
        cotangent, in_sems = staged[2].at[number_of_block], in_sems_all.at[number_of_block]
        tokens_copy = pltpu.make_async_copy(
            tokens_hbm.at[pl.ds(block * rows, rows), :], tokens, in_sems.at[0]
        )
        tokens_copy.start()
        lanes = pl.ds(block * members * each, members * each)
        context_copies, cotangent_copies = [], []
        for number, ((distance, half), piece) in enumerate(zip(kinds, pieces)):
            if half != 0:
                first = span if half is None else 0
                context_copies.append(
                    pltpu.make_async_copy(
                        piece.at[pl.ds(first, span), lanes],
                        context.at[distance],
                        in_sems.at[1 + 2 * number],
                    )
                )
                context_copies[-1].start()
        for number, ((distance, half), piece) in enumerate(zip(kinds, pieces)):
            if half != 1:
                owner = meta[seqs + distance]
                inside = owner // members == block
                start = pl.multiple_of(
                    jnp.where(inside, owner - block * members, 0) * span, 16
                )
                copy = pltpu.make_async_copy(
                    piece.at[pl.ds(0, span), :],
                    cotangent.at[pl.ds(start, span), :],
                    in_sems.at[2 + 2 * number],
                )
                pl.when(inside)(copy.start)
                cotangent_copies.append((inside, copy))
        return tokens_copy, context_copies, cotangent_copies

    def work(number_of_block, block, brought, staged):
        tokens_copy, context_copies, cotangent_copies = brought
        staged = [ref.at[number_of_block] for ref in staged]
        heads_out, mix_out, tokens, context = (
            ref.at[number_of_block] for ref in (heads_all, mix_all, tokens_all, context_all)
        )
        sems = sems_all.at[number_of_block]
        at_row = seq * seq_len + block * rows
        lanes = pl.ds(block * members * each, members * each)
        (
            context_out,
            normed_out,
            cotangent,
            hidden_out,
            grad_gate_out,
            grad_up_out,
            grad_out,
            logits_out,
        ) = staged
        copies = [
            pltpu.make_async_copy(source, target.at[pl.ds(at_row, rows), :], sems.at[number])
            for number, (source, target) in enumerate(zip(staged, buffers))
        ]
        heads_copy = pltpu.make_async_copy(
            heads_out, sums_out.at[:, pl.ds(0, span), lanes], sems.at[8]
        )
        mix_copies = [
            pltpu.make_async_copy(
                mix_out.at[pl.ds(part * span, span), :],
                sums_out.at[meta[seqs + count + block * members + part], pl.ds(span, span), :],
                sems.at[9 + part],
            )
            for part in range(members)
        ]

        group = seqs * span
        before = (
            lax.broadcasted_iota(jnp.int32, (group, group), 0)
            < lax.broadcasted_iota(jnp.int32, (group, group), 1)
        ).astype(bf16)
        expert_row = lax.broadcasted_iota(jnp.int32, (8, group), 0).astype(f32)
        member_lane = lax.broadcasted_iota(jnp.int32, (1, group), 1)
        codes = []
        for part in range(members):
            owner = block * members + part
            line = ids[pl.ds(meta[seqs + count + owner], 1), :]
            alive = jnp.zeros((1, group), f32)
            for other in range(seqs):
                inside = jnp.logical_and(
                    member_lane >= other * span, member_lane < (other + 1) * span
                )
                inside = jnp.logical_and(
                    inside, member_lane - other * span + owner * span < meta[other]
                )
                alive = jnp.where(inside, 1.0, alive)
            taken = jnp.logical_or(
                line[:, :group] == expert_row, line[:, group : 2 * group] == expert_row
            ).astype(f32)
            earlier = dot_nn((taken * alive).astype(bf16), before)
            code = taken * (1.0 + jnp.where(earlier < capacity, alive, 0.0))
            code = code[:, seq * span : (seq + 1) * span]
            code = jnp.concatenate([code, jnp.zeros((120, span), f32)], axis=0)
            codes.append(code.T)
        code = jnp.concatenate(codes, axis=0)

        total_units = gate_weight.shape[0]
        units = total_units // expert_count
        cuts = [slice(i, min(i + 256, total_units)) for i in range(0, total_units, 256)]
        row = block * rows + lax.broadcasted_iota(jnp.int32, (rows, 1), 0)
        own = jnp.logical_and(row >= me * span, row < (me + 1) * span)
        for copy in context_copies:
            copy.wait()
        joined = jnp.concatenate(
            [
                jnp.concatenate(
                    [context[d, :, part * each : (part + 1) * each] for d in range(count)], axis=1
                )
                for part in range(members)
            ],
            axis=0,
        )
        context_out[...] = joined
        copies[0].start()
        tokens_copy.wait()
        hidden = tokens[...].astype(f32) + dot_nn(joined, out_weight[...])
        factor = lax.rsqrt(jnp.mean(hidden * hidden, axis=-1, keepdims=True) + epsilon)
        normed = (hidden * factor * gain[...]).astype(bf16)
        normed_out[...] = normed
        copies[1].start()
        logits = dot_nn(normed, router_weight[...])
        lane = lax.broadcasted_iota(jnp.int32, logits.shape, 1)
        logits = jnp.where(lane < expert_count, logits, -1e30)
        router = jnp.exp(logits - jnp.max(logits, axis=-1, keepdims=True))
        router = router / jnp.sum(router, axis=-1, keepdims=True)
        chosen = (code > 0.5).astype(f32)
        kept = (code > 1.5).astype(f32)
        pair_total = jnp.sum(router * chosen, axis=-1, keepdims=True)
        share = router * chosen / pair_total
        scale = share * kept
        for inside, copy in cotangent_copies:
            pl.when(inside)(copy.wait)
        copies[2].start()
        upstream = jnp.where(row < length, cotangent[...].astype(f32), 0.0)
        upstream_low = upstream.astype(bf16)
        root = 0.7978845608028654
        pair_grads = jnp.zeros(logits.shape, f32)
        scale_of = [jnp.broadcast_to(scale[:, e : e + 1], (rows, 128)) for e in range(expert_count)]
        part_sums = [jnp.zeros((rows, 128), f32) for e in range(expert_count)]
        lanes = lax.broadcasted_iota(jnp.int32, (rows, 128), 1)

        def front(number):
            cut = cuts[number]
            return (
                dot_nt(normed, gate_weight[cut, :]),
                dot_nt(normed, up_weight[cut, :]),
                dot_nt(upstream_low, down_weight[cut, :]),
            )

        ready = front(0)
        for number, cut in enumerate(cuts):
            now = ready
            if number + 1 < len(cuts):
                ready = front(number + 1)
            for first in range(cut.start, cut.stop, 128):
                wide = min(128, cut.stop - first)
                inside = slice(first - cut.start, first - cut.start + wide)
                gate_in, up_in, grad_hidden = (value[:, inside] for value in now)
                square = gate_in * gate_in
                bent = gate_in * (root + (root * 0.044715) * square)
                rise = 0.5 + 0.5 * jnp.tanh(bent)
                gelu = gate_in * rise
                slope = rise + (rise - rise * rise) * (6.0 * bent - (4.0 * root) * gate_in)
                hidden_unit = gelu * up_in
                product = hidden_unit * grad_hidden
                low_expert, high_expert = first // units, (first + wide - 1) // units
                scales = scale_of[low_expert][:, :wide]
                if low_expert == high_expert:
                    if wide < 128:
                        product = jnp.pad(product, ((0, 0), (0, 128 - wide)))
                    part_sums[low_expert] = part_sums[low_expert] + product
                else:
                    under = lanes[:, :wide] < high_expert * units - first
                    scales = jnp.where(under, scales, scale_of[high_expert][:, :wide])
                    part_sums[low_expert] = part_sums[low_expert] + jnp.where(under, product, 0.0)
                    part_sums[high_expert] = part_sums[high_expert] + jnp.where(under, 0.0, product)
                scaled_grad = scales * grad_hidden
                at = slice(first, first + wide)
                hidden_out[:, at] = (scales * hidden_unit).astype(bf16)
                grad_gate_out[:, at] = (scaled_grad * up_in * slope).astype(bf16)
                grad_up_out[:, at] = (scaled_grad * gelu).astype(bf16)
        for expert in range(expert_count):
            pair_sum = jnp.sum(part_sums[expert], axis=-1, keepdims=True)
            pair_grads = jnp.where(lane == expert, pair_sum, pair_grads)
        for copy in copies[3:6]:
            copy.start()
        mix = dot_nn(hidden_out[...], down_weight[...])
        grad = dot_nn(grad_gate_out[...], gate_weight[...]) + dot_nn(grad_up_out[...], up_weight[...])
        mix_out[...] = (mix + jnp.where(own, hidden, 0.0)).astype(bf16)
        for copy in mix_copies:
            copy.start()
        pair_grads = pair_grads * kept
        weighted = jnp.sum(pair_grads * share, axis=-1, keepdims=True)
        grad_router = chosen * (pair_grads - weighted) / pair_total
        grad_logits = router * (grad_router - jnp.sum(router * grad_router, axis=-1, keepdims=True))
        grad_logits = grad_logits.astype(bf16)
        logits_out[...] = grad_logits
        copies[7].start()
        grad = grad + dot_nt(grad_logits, router_weight[...])
        spread = hidden * factor
        gain_part = jnp.sum(grad * spread, axis=0, keepdims=True)
        if number_of_block == 0:
            gain_out[...] = gain_in[...]
        gain_out[0:1, :] += gain_part
        grad = grad * gain[...]
        middle = jnp.mean(grad * hidden, axis=-1, keepdims=True) * (factor * factor)
        back = factor * grad - spread * middle + jnp.where(own, upstream, 0.0)
        back = back.astype(bf16)
        grad_out[...] = back
        copies[6].start()
        grad_heads = dot_nt(back, out_weight[...]).astype(bf16)
        for d in range(count):
            for part in range(members):
                heads_out[d, :, part * each : (part + 1) * each] = grad_heads[
                    part * span : (part + 1) * span, d * each : (d + 1) * each
                ]
        heads_copy.start()
        return [*copies, *mix_copies, heads_copy]

    brought = [bring(number, block) for number, block in enumerate(blocks)]
    started = []
    for number, block in enumerate(blocks):
        started += work(number, block, brought[number], staged)
    for copy in started:
        copy.wait()


def experts(
    meta,
    where,
    tokens,
    pieces,
    gain,
    router_weight,
    ids,
    gain_in,
    weights,
    buffers,
    sums,
    sizes,
):
    seq, blocks = where
    count, span, seqs, expert_count, capacity = sizes
    seq_len, width = tokens.shape
    units = weights[1].shape[0]
    rows = 256
    each = width // count
    members = rows // span
    many = len(blocks)
    kinds = [(d, half) for d, half, piece in pieces]
    anywhere = pl.BlockSpec(memory_space=pl.ANY)
    low = lambda *shape: jax.ShapeDtypeStruct(shape, bf16)
    columns = [width] * 3 + [units] * 3 + [width, 128]
    aliased = list(buffers or []) + ([sums] if sums is not None else [])
    first = 2 + len(pieces) + 8
    targets = ([*range(8)] if buffers else []) + ([8] if sums is not None else [])
    static = (count, span, seqs, expert_count, capacity, seq, blocks, kinds, len(aliased))
    return pl.pallas_call(
        functools.partial(experts_kernel, static),
        out_shape=[low(seqs * seq_len, cols) for cols in columns]
        + [low(count, 2 * span, width), jax.ShapeDtypeStruct((8, width), f32)],
        in_specs=[pl.BlockSpec(memory_space=pltpu.SMEM)]
        + [anywhere] * (1 + len(pieces))
        + [whole_ref] * 8
        + [anywhere] * len(aliased),
        out_specs=[anywhere] * 9 + [whole_ref],
        scratch_shapes=[pltpu.VMEM((many, rows, cols), bf16) for cols in columns]
        + [
            pltpu.VMEM((many, count, span, members * each), bf16),
            pltpu.VMEM((many, rows, width), bf16),
            pltpu.VMEM((many, rows, width), bf16),
            pltpu.VMEM((many, count, span, members * each), bf16),
            pltpu.SemaphoreType.DMA((many, 9 + members)),
            pltpu.SemaphoreType.DMA((many, 1 + 2 * len(pieces))),
        ],
        input_output_aliases={first + i: target for i, target in enumerate(targets)},
        compiler_params=pltpu.CompilerParams(vmem_limit_bytes=36 * 2**20),
        cost_estimate=pl.CostEstimate(
            flops=2 * many * rows * width * (6 * units + 2 * width),
            bytes_accessed=1000,
            transcendentals=many * rows * units,
        ),
        name="experts",
    )(
        meta,
        tokens,
        *[piece for d, half, piece in pieces],
        gain,
        router_weight,
        ids,
        gain_in,
        *weights,
        *aliased,
    )


def block_sets(blocks, seq):
    step = 1 if seq == 0 else 2
    return [list(range(i, min(i + step, blocks))) for i in range(0, blocks, step)]


def attend_back_kernel(seq, head, heads, meta, queries_in, keys_in, values_in, *refs):
    own, right, left, bias, parts_out, sums_out = refs[:6]
    table, key_sum, value_sum, summed = refs[6:]
    length = meta[seq]
    _, seq_len, head_size = keys_in.shape
    span = right.shape[0]
    each = heads * head_size
    blocks = seq_len // 128
    summed[...] = (own[0].astype(f32) + right[...].astype(f32) + left[...].astype(f32)).astype(bf16)
    table[...] = jnp.zeros_like(table)
    keys = keys_in[0]
    values = values_in[0]
    for block in range(0, blocks, 2):
        rows = slice(block * 128, block * 128 + 256)
        queries = queries_in[0, rows, :]
        firsts = [
            part * each + head * head_size
            for part in range(block * 128 // span, (block * 128 + 256) // span)
        ]
        grads = jnp.concatenate(
            [summed[:, lane : lane + head_size] for lane in firsts], axis=0
        )
        first_row = (blocks - 1 - block) * 128
        added = jnp.concatenate(
            [
                bias[0, first_row : first_row + seq_len, :],
                bias[0, first_row - 128 : first_row - 128 + seq_len, :],
            ],
            axis=1,
        )
        scores = dot_nt(keys, queries)
        row = lax.broadcasted_iota(jnp.int32, scores.shape, 0)
        scores = jnp.where(row < length, scores + added, -1e30)
        top = jnp.max(scores, axis=0, keepdims=True)
        probs = jnp.exp(scores - top)
        probs = probs * (1.0 / jnp.sum(probs, axis=0, keepdims=True))
        product = probs * dot_nt(values, grads)
        delta = jnp.sum(product, axis=0, keepdims=True)
        grad_scores = product - probs * delta
        table[first_row : first_row + seq_len, :] += grad_scores[:, :128]
        table[first_row - 128 : first_row - 128 + seq_len, :] += grad_scores[:, 128:]
        scores_low = grad_scores.astype(bf16)
        key_part = dot_nn(scores_low, queries)
        value_part = dot_nn(probs.astype(bf16), grads)
        if block == 0:
            key_sum[...] = key_part
            value_sum[...] = value_part
        else:
            key_sum[...] += key_part
            value_sum[...] += value_part
        query_grad = dot_tn(keys, scores_low) * head_size ** (-0.5)
        parts_out[0, rows, :] = query_grad.T.astype(bf16)
    parts_out[1] = key_sum[...].astype(bf16)
    parts_out[2] = value_sum[...].astype(bf16)
    width = table.shape[0] + 128
    lines = jnp.concatenate(
        [table[first : first + 128, :].T for first in range(0, width - 128, 128)]
        + [jnp.zeros((128, 128), f32)],
        axis=1,
    )
    rows = 128
    while rows > 1:
        rows //= 2
        lines = lines[:rows] + pltpu.roll(lines[rows : 2 * rows], width - rows, 1)
    sums_out[...] = jnp.broadcast_to(pltpu.roll(lines, 127, 1), sums_out.shape)


def attend_back(meta, seq, head, heads, qkv, own, right, left, span, bias):
    _, seq_len, head_size = qkv.shape
    width = right.shape[1]
    part = lambda at: pl.BlockSpec((1, seq_len, head_size), lambda i, meta: (at, 0, 0))
    full = lambda *shape: pl.BlockSpec(shape, lambda i, meta: (0,) * len(shape))
    low = jax.ShapeDtypeStruct((3, seq_len, head_size), bf16)
    return pl.pallas_call(
        functools.partial(attend_back_kernel, seq, head, heads),
        out_shape=(low, jax.ShapeDtypeStruct((8, 2 * seq_len), f32)),
        grid_spec=pltpu.PrefetchScalarGridSpec(
            num_scalar_prefetch=1,
            grid=(1,),
            in_specs=[part(head), part(heads + head), part(2 * heads + head)]
            + [full(1, span, width), full(span, width), full(span, width)]
            + [pl.BlockSpec((1,) + bias.shape[1:], lambda i, meta: (head, 0, 0))],
            out_specs=[full(3, seq_len, head_size), full(8, 2 * seq_len)],
            scratch_shapes=[
                pltpu.VMEM(bias.shape[1:], f32),
                pltpu.VMEM((seq_len, head_size), f32),
                pltpu.VMEM((seq_len, head_size), f32),
                pltpu.VMEM((span, width), bf16),
            ],
        ),
        compiler_params=pltpu.CompilerParams(vmem_limit_bytes=28 * 2**20),
        cost_estimate=pl.CostEstimate(
            flops=6 * 10**9, bytes_accessed=1000, transcendentals=seq_len * seq_len
        ),
        name="attend_back",
    )(meta, qkv, qkv, qkv, own, right, left, bias)


def norm_back_kernel(heads, first, meta, *refs):
    parts, (tokens, weight, grad_in, grad_out, parts_out, gain_out) = refs[:heads], refs[heads:]

    @pl.when(pl.program_id(0) == 0)
    def _():
        gain_out[...] = jnp.zeros_like(gain_out)

    low = jnp.concatenate([part[kind] for kind in range(3) for part in parts], axis=1)
    wide = tokens[...].astype(f32)
    factor = lax.rsqrt(jnp.mean(wide * wide, axis=-1, keepdims=True) + epsilon)
    upstream = dot_nt(low, weight[...])
    spread = wide * factor
    gain_out[0:1, :] += jnp.sum(upstream * spread, axis=0, keepdims=True)
    middle = jnp.mean(upstream * wide, axis=-1, keepdims=True) * (factor * factor)
    back = factor * upstream - spread * middle + grad_in[...].astype(f32)
    back = back.astype(bf16)
    span = grad_out.shape[1]
    members = back.shape[0] // span
    for part in range(members):
        distance = meta[first + pl.program_id(0) * members + part]
        grad_out[distance] = back[part * span : (part + 1) * span, :]
    parts_out[...] = (low.astype(f32) * factor).astype(bf16)


def norm_back(meta, seq, seqs, parts, tokens, weight, grad_in, count):
    seq_len, width = tokens.shape
    head_size = parts[0].shape[2]
    rows, span = 256, seq_len // count
    by_row = lambda cols, at=0: pl.BlockSpec((rows, cols), lambda i, meta: (at + i, 0))
    columns = 3 * head_size * len(parts)
    return pl.pallas_call(
        functools.partial(norm_back_kernel, len(parts), seqs + count),
        out_shape=(
            jax.ShapeDtypeStruct((count, span, width), bf16),
            jax.ShapeDtypeStruct((seq_len, columns), bf16),
            jax.ShapeDtypeStruct((8, width), f32),
        ),
        grid_spec=pltpu.PrefetchScalarGridSpec(
            num_scalar_prefetch=1,
            grid=(seq_len // rows,),
            in_specs=[pl.BlockSpec((3, rows, head_size), lambda i, meta: (0, i, 0))] * len(parts)
            + [
                by_row(width),
                pl.BlockSpec(weight.shape, lambda i, meta: (0, 0)),
                by_row(width, seq * (seq_len // rows)),
            ],
            out_specs=(
                pl.BlockSpec((count, span, width), lambda i, meta: (0, 0, 0)),
                by_row(columns),
                pl.BlockSpec((8, width), lambda i, meta: (0, 0)),
            ),
        ),
        compiler_params=pltpu.CompilerParams(vmem_limit_bytes=24 * 2**20),
        cost_estimate=pl.CostEstimate(
            flops=2 * seq_len * width * columns, bytes_accessed=1000, transcendentals=0
        ),
        name="norm_back",
    )(meta, *parts, tokens, weight, grad_in)


def spread_kernel(reps, spots, *refs):
    parts, gain, outs = refs[:reps], refs[reps], refs[reps + 1 :]
    count, _, columns = parts[0].shape
    cut = gain.shape[0] // reps
    each = columns // 3
    for number, part in enumerate(parts):
        rows = pl.ds(pl.multiple_of(spots[number] * cut, cut), cut)
        scale = gain[rows, :]
        for owner in range(count):
            block = part[owner, :cut, :].astype(f32) * scale
            for kind, out in enumerate(outs):
                out[rows, owner * each : (owner + 1) * each] = block[:, kind * each : (kind + 1) * each]


def spread(parts, spots, found, gain):
    count, _, columns = parts[0].shape
    cut, each = gain.shape[0] // len(parts), columns // 3
    if cut % 8:
        whole = jnp.take(jnp.stack(parts), found, axis=0)[:, :, :cut].astype(f32)
        whole = whole.reshape(len(parts), count, cut, 3, each).transpose(3, 0, 2, 1, 4)
        whole = whole.reshape(3, gain.shape[0], count * each) * gain[None, :, None]
        return whole[0], whole[1], whole[2]
    shape = jax.ShapeDtypeStruct((gain.shape[0], count * each), f32)
    return pl.pallas_call(
        functools.partial(spread_kernel, len(parts)),
        out_shape=(shape,) * 3,
        in_specs=[pl.BlockSpec(memory_space=pltpu.SMEM)] + [whole_ref] * (len(parts) + 1),
        out_specs=[whole_ref] * 3,
        compiler_params=pltpu.CompilerParams(vmem_limit_bytes=12 * 2**20),
        name="spread",
    )(spots, *parts, gain.reshape(-1, 1))


def body(
    tokens,
    lengths,
    expert_ids,
    buckets,
    norm1_gain,
    w_query,
    w_key,
    w_value,
    w_out,
    rel_bias,
    norm2_gain,
    w_router,
    w_gate,
    w_up,
    w_down,
    cotangent,
):
    seqs, span, width = tokens.shape
    count = lax.axis_size("shard")
    reps = lax.axis_size("rep")
    me = lax.axis_index("shard")
    rep = lax.axis_index("rep")
    seq_len = span * count
    expert_count, unit_count, _ = w_gate.shape
    heads = rel_bias.shape[1]
    head_size = w_query.shape[1] // (count * heads)
    each = heads * head_size
    feats = w_query.shape[0]
    cut = feats // reps
    row_count = seqs * span
    capacity = 10 * row_count // (4 * expert_count)
    place = ring_place(me, count)
    distances = jnp.arange(count, dtype=jnp.int32)
    owners = ring_index((place + distances) % count, count)
    distance_of = (ring_place(distances, count) - place) % count
    meta = jnp.concatenate([lengths, owners, distance_of, me[None]]).astype(jnp.int32)

    def line(values):
        flat = values.reshape(-1).astype(bf16)
        return jnp.pad(flat, (0, width - flat.shape[0]))[None]

    packed = jnp.concatenate(
        [
            tokens.reshape(row_count, width),
            lax.dynamic_slice_in_dim(w_out, rep * cut, cut, 0),
            line(expert_ids.reshape(row_count, 2).T),
            line(jnp.concatenate([norm2_gain, w_router.reshape(-1)])),
            jnp.zeros((14, width), bf16),
        ],
        axis=0,
    )
    extra = row_count
    token_ring = Gather(
        packed,
        count,
        lambda value: (
            jnp.concatenate([value[:span], value[extra:]], axis=0),
            value[span:extra],
        ),
    )
    hops = []
    while not token_ring.done:
        fire([token_ring])
        hops.append(token_ring.last())

    gain_one = norm1_gain.astype(f32)
    own_qkv = jnp.stack([w_query, w_key, w_value], axis=1)
    own_cut = lax.dynamic_slice_in_dim(own_qkv, rep * cut, cut, 0).astype(f32)
    own_cut = own_cut * lax.dynamic_slice_in_dim(gain_one, rep * cut, cut, 0)[:, None, None]
    own_cut = own_cut.astype(bf16).reshape(cut, 3, count, each).transpose(2, 0, 1, 3)
    qkv_weight = lax.all_to_all(
        own_cut.reshape(count, cut, 3 * each), "shard", split_axis=0, concat_axis=0, tiled=True
    )
    qkv_weight = weave(*rep_parts(after(qkv_weight, hops[1]), reps, rep))

    bucket_count = rel_bias.shape[0]
    bucket_hot = (
        buckets[:, None] == jnp.arange(bucket_count, dtype=jnp.int32)[None, :]
    ).astype(f32)
    bucket_hot = jnp.pad(bucket_hot, ((0, 1), (0, 0)))
    bias_vec = jnp.einsum("rb,bh->hr", bucket_hot, rel_bias.astype(f32), precision=highest)
    bias, bias_turned = bias_tables(bias_vec)

    def sent(rings):
        return tuple(ring.last() for ring in rings if ring.last()[0] is not None)

    attended, mixed_rings, rings = [], [], []
    waits = token_ring.last()
    for s in range(seqs):
        fire(rings, waits)
        attended.append(
            attend(
                after(meta, waits),
                s,
                seqs,
                token_ring.pieces,
                cotangent[s],
                qkv_weight,
                bias,
                heads,
                head_size,
            )
        )
        waits = (attended[s][2], sent(rings))
        if s == 0:
            riders = attended[s][3]
            out_parts = rep_parts(riders[:, :cut], reps, rep)
        mixed_rings.append(Gather(attended[s][2], count))
        rings = [mixed_rings[0]]
    while not rings[0].done:
        fire(rings, waits)
        waits = lasts(rings)

    out_weight = weave(*out_parts)
    ids = riders[:, cut].astype(f32)
    small = jnp.take(riders[:, cut + 1], distance_of, axis=0)
    gain_two = small[:, :feats].astype(f32).reshape(1, width)
    router_weight = small[:, feats : feats * (1 + expert_count)].reshape(width, expert_count)
    router_weight = jnp.pad(router_weight, ((0, 0), (0, 128 - expert_count)))
    expert_weights = [out_weight] + [
        weight.reshape(expert_count * unit_count, width) for weight in (w_gate, w_up, w_down)
    ]

    sizes = (count, span, seqs, expert_count, capacity)
    buffers = None
    gain_part = jnp.zeros((8, width), f32)
    sums_all, sum_rings = [], []
    rings = [mixed_rings[1]]
    for s in range(seqs):
        if s > 0:
            while not rings[0].done:
                fire(rings, waits)
                waits = lasts(rings)
            sum_rings.append(Sum([(sums_all[s - 1], 0, 2 * span)], count))
            rings = [sum_rings[s - 1]]
        sums = None
        for blocks in block_sets(seq_len // 256, s):
            if not rings[0].done:
                fire(rings, waits)
            *buffers, sums, gain_part = experts(
                after(meta, waits),
                (s, blocks),
                attended[s][0],
                mixed_rings[s].pieces,
                gain_two,
                router_weight,
                ids,
                gain_part,
                expert_weights,
                buffers,
                sums,
                sizes,
            )
            waits = (gain_part, sent(rings))
        sums_all.append(sums)
    context_rows, normed, cot_rows, hidden, grad_gate, grad_up, grad_rows, grad_logits = buffers

    offset_sums, totals, finished, scaled_all, gain_one_part = [], [], [], [], []

    def total_grad(left_side, right_side, waits):
        grads = dot_tn(after(left_side, waits), right_side).astype(bf16)
        totals.append(RepTotal(grads, reps, rep))
        return grads

    def step(rings, waits):
        live = [ring for ring in rings if not ring.done]
        if live:
            fire(live, waits)

    def back_head(s, head, waits):
        made = attend_back(
            after(meta, waits),
            s,
            head,
            heads,
            attended[s][1],
            sums_all[s],
            *sum_rings[s].last(),
            span,
            bias_turned,
        )
        offset_sums.append((head, made[1]))
        return made[0]

    def back_norm(s, parts, waits):
        grads, scaled, gain_rows = norm_back(
            after(meta, waits), s, seqs, parts, attended[s][0], qkv_weight, grad_rows, count
        )
        scaled_all.append(scaled)
        gain_one_part.append(gain_rows)
        return grads

    sum_rings.append(Sum([(sums_all[1], 0, 2 * span)], count))
    first, second = sum_rings
    rings = [first]
    step(rings, waits)
    done = total_grad(hidden, cot_rows, waits)
    rings = [first, second]
    waits = (done, sent(rings))
    step(rings, waits)
    out_grad = dot_tn(after(context_rows, waits), grad_rows).astype(bf16)
    router_grad = dot_tn(normed, grad_logits)[:, :expert_count]
    flat = jnp.concatenate(
        [gain_part[0].reshape(count, feats), router_grad.reshape(count, feats * expert_count)], axis=1
    ).astype(bf16)
    flat = jnp.take(flat, owners, axis=0)
    small_size = flat.shape[1] // 2
    flat = jnp.pad(flat.reshape(count, 2, 1, small_size), ((0, 0), (0, 0), (0, 15), (0, width - small_size)))
    out_whole = jnp.concatenate([out_grad.reshape(count, 2, each // 2, width), flat], axis=2)
    side = rep % 2
    out_kept = lax.dynamic_index_in_dim(out_whole, side, 1, keepdims=False)
    out_got = swap(lax.dynamic_index_in_dim(out_whole, 1 - side, 1, keepdims=False), "rep", reps, 1)
    done = total_grad(grad_gate, normed, (waits, out_grad))
    waits = (done, sent(rings))
    while not first.done:
        step(rings, waits)
        waits = lasts(rings)
    rings = [second]
    parts = []
    for head in range(heads):
        step(rings, waits)
        parts.append(back_head(0, head, waits))
        waits = (parts[-1], sent(rings))
        if head == 0:
            totals[0].cross()
            out_grad = add_low(out_kept, out_got)
            waits = waits + (totals[0].kept, out_grad)
    totals[1].cross()
    waits = waits + (totals[1].kept,)
    grads_first = back_norm(0, parts, waits)
    waits = (grads_first, waits)
    final = [Sum([(grads_first, 0, span), (out_grad, 0, out_grad.shape[1])], count)]
    rings = [second, final[0]]
    step(rings, waits)
    done = total_grad(grad_up, normed, (waits, totals[0].got))
    waits = (done, sent(rings))
    while not second.done:
        step(rings, waits)
        waits = lasts(rings)
    rings = [final[0]]
    parts = []
    for head in range(heads):
        step(rings, waits)
        parts.append(back_head(1, head, waits))
        waits = (parts[-1], sent(rings))
        if head == 0:
            totals[2].cross()
            waits = waits + (totals[2].kept, totals[1].got)
    step(rings, waits)
    grads_last = back_norm(1, parts, waits)
    final.append(Sum([(grads_last, 0, span)], count))
    waits = (grads_last, sent(rings))
    rings = final
    while not all(ring.done for ring in rings):
        step(rings, waits)
        waits = lasts(rings)

    mix_first, mix_last, final_first, final_last = (
        ring.total() for ring in (*sum_rings, *final)
    )
    grad_tokens = jnp.stack([final_first[:span], final_last])
    positions = me * span + jnp.arange(span, dtype=jnp.int32)
    live_mask = (positions[None, :] < lengths[:, None]).astype(f32)[:, :, None]
    block_out = (live_mask * jnp.stack([mix_first[span:], mix_last[span:]])).astype(bf16)
    out_own = final_first[span:].astype(bf16)
    for bit in bits_of(reps)[1:]:
        out_own = add_low(out_own, swap(out_own, "rep", reps, bit))
    out_other = swap(out_own, "rep", reps, 1)
    out_both = jnp.where(
        side == 0, jnp.stack([out_own, out_other]), jnp.stack([out_other, out_own])
    ).astype(f32)
    total_out = out_both[:, : each // 2].reshape(feats, width)
    flat = out_both[:, each // 2, :small_size].reshape(-1)
    total_gain_two = flat[:feats]
    total_router = flat[feats:].reshape(feats, expert_count)

    qkv_grad = sum(dot_tn(attended[s][0], scaled_all[s]) for s in range(seqs)).astype(bf16)
    offsets = jnp.stack(
        [sum(part[0] for h, part in offset_sums if h == head) for head in range(heads)]
    )
    bias_grad = jnp.einsum("hr,rb->hb", offsets, bucket_hot, precision=highest)
    gain_rows = sum(part[0] for part in gain_one_part).reshape(count, reps, 1, cut)
    bias_rows = jnp.broadcast_to(
        bias_grad.reshape(1, reps, 1, -1), (count, reps, 1, bias_grad.size // reps)
    )
    flat = jnp.concatenate([gain_rows, bias_rows], axis=3).astype(bf16)
    flat = jnp.pad(flat, ((0, 0), (0, 0), (0, 15), (0, 3 * each - flat.shape[3])))
    qkv_grad = jnp.concatenate([qkv_grad.reshape(count, reps, cut, 3 * each), flat], axis=2)
    qkv_grad = rep_scatter(qkv_grad.transpose(1, 0, 2, 3), reps, rep, totals[2].got)
    qkv_grad = lax.all_to_all(qkv_grad, "shard", split_axis=0, concat_axis=0, tiled=True)
    bias_size = bias_grad.size // reps
    parts, spots = rep_parts(qkv_grad, reps, rep)
    found = jnp.take(jnp.array(rep_order(reps), jnp.int32), rep ^ jnp.arange(reps))
    qkv_grad = spread(parts, spots, found, gain_one)
    tail = jnp.take(jnp.stack([part[:, cut] for part in parts]), found, axis=0).astype(f32)
    total_gain_one = jnp.sum(tail[:, :, :cut], axis=1).reshape(feats) / gain_one
    total_bias = lax.dynamic_index_in_dim(tail, me, 1, keepdims=False)[:, cut : cut + bias_size]
    total_bias = total_bias.reshape(heads, bucket_count).T

    total_down, total_gate, total_up = (
        total.finish().reshape(expert_count, unit_count, width) for total in totals
    )
    return (
        block_out,
        grad_tokens,
        total_gain_one,
        qkv_grad[0],
        qkv_grad[1],
        qkv_grad[2],
        total_out,
        total_bias,
        total_gain_two,
        total_router,
        total_gate,
        total_up,
        total_down,
    )


def solution(mesh):
    rows = P("rep", "shard", None)
    first = P("shard")
    weight = P("shard", None)
    expert = P(None, "shard", None)
    return jax.shard_map(
        body,
        mesh=mesh,
        in_specs=(rows, P("rep"), rows, P(), first, weight, weight, weight, weight)
        + (P(None, "shard"), first, weight, expert, expert, expert, rows),
        out_specs=(rows, rows, first, weight, weight, weight, weight)
        + (P(None, "shard"), first, weight, expert, expert, expert),
        check_vma=False,
    )
```

profile of v0, /device:TPU:1, one launch (start us, length us, event | category | flops | bytes accessed | tf_op | source)
XLA Modules:
  0.0 488.0 jit_solution(13551034657376908692)
XLA Ops:
  7.4 13.7 %collective-permute-done.refs_1_ = bf16[304,1024]{1,0:T(8,128)(2,1)S(1)} collective-permute-done((bf16[304,1024]{1,0:T(8,128)(2,1)S(1)}, bf16[304,1024]{1,0:T(8,128)(2,1)S(1)}, u32[]{:S(2)}, u32[]{:S(2)}) %collective-permute-start) | collective-permute-done | bytes 622624 | tf_op jit(solution)/shard_map/ppermute | solution.py:41
  26.3 4.6 all-to-all-start
  30.9 4.9 collective-permute-done.2.refs_3_
  41.7 8.2 %collective-permute-done.4.refs_5_ = bf16[304,1024]{1,0:T(8,128)(2,1)S(1)} collective-permute-done((bf16[304,1024]{1,0:T(8,128)(2,1)}, bf16[304,1024]{1,0:T(8,128)(2,1)S(1)}, u32[]{:S(2)}, u32[]{:S(2)}) %collective-permute-start.4) | collective-permute-done | bytes 622624 | tf_op jit(solution)/shard_map/ppermute | solution.py:41
  50.9 4.0 collective-permute-start.6
  57.6 4.0 collective-permute-start.9
  66.2 8.0 %attend.2 = (bf16[1024,1024]{1,0:T(8,128)(2,1)S(1)}, bf16[6,1024,64]{2,1,0:T(8,128)(2,1)S(1)}, bf16[256,1024]{1,0:T(8,128)(2,1)S(1)}, bf16[8,48,1024]{2,1,0:T(8,128)(2,1)S(1)}) custom-call(s32[19]{0:T(128)S(1)} %pad_add_fusion.meta, bf16[304,1024]{1,0:T(8,128)(2,1)S(1)} %concatenate.44.refs_0_, bf16[304,1024]{1,0:T(8,128)(2,1)S(1)} %copy-done.92, ...), custom_call_target="tpu_custom_call" | custom-call | flops 8000000000 | bytes 1000 | tf_op jit(solution)/shard_map/attend/pallas_call | solution.py:430
  78.7 7.6 %attend.3 = (bf16[1024,1024]{1,0:T(8,128)(2,1)S(1)}, bf16[6,1024,64]{2,1,0:T(8,128)(2,1)S(1)}, bf16[256,1024]{1,0:T(8,128)(2,1)S(1)}) custom-call(s32[19]{0:T(128)S(1)} %pad_add_fusion.meta, bf16[304,1024]{1,0:T(8,128)(2,1)S(1)} %concatenate.44.refs_0_, bf16[304,1024]{1,0:T(8,128)(2,1)S(1)} %copy-done.92, bf16[304,1024]{1,0:T(8,128)(2,1)S(1)} %copy-done.94, ...), custom_call_target="tpu_custom_call" | custom-call | flops 8000000000 | bytes 1000 | tf_op jit(solution)/shard_map/attend/pallas_call | solution.py:430
  95.2 8.3 %collective-permute-done.13.refs_4_ = bf16[256,1024]{1,0:T(8,128)(2,1)S(1)} collective-permute-done((bf16[256,1024]{1,0:T(8,128)(2,1)S(1)}, bf16[256,1024]{1,0:T(8,128)(2,1)S(1)}, u32[]{:S(2)}, u32[]{:S(2)}) %collective-permute-start.13) | collective-permute-done | bytes 524320 | tf_op jit(solution)/shard_map/ppermute | solution.py:41
  109.5 4.9 %collective-permute-done.15.refs_6_ = bf16[256,1024]{1,0:T(8,128)(2,1)S(1)} collective-permute-done((bf16[256,1024]{1,0:T(8,128)(2,1)S(1)}, bf16[256,1024]{1,0:T(8,128)(2,1)S(1)}, u32[]{:S(2)}, u32[]{:S(2)}) %collective-permute-start.15) | collective-permute-done | bytes 524320 | tf_op jit(solution)/shard_map/ppermute | solution.py:41
  135.0 10.6 %experts.6 = (bf16[2048,1024]{1,0:T(8,128)(2,1)}, bf16[2048,1024]{1,0:T(8,128)(2,1)}, bf16[2048,1024]{1,0:T(8,128)(2,1)}, bf16[2048,1408]{1,0:T(8,128)(2,1)}, bf...) custom-call(s32[19]{0:T(128)S(1)} %pad_add_fusion.meta, ...), custom_call_target="tpu_custom_call" | custom-call | flops 5502926848 | bytes 1000 | tf_op jit(solution)/shard_map/experts/pallas_call | solution.py:727
  147.1 10.6 %experts.7 = (bf16[2048,1024]{1,0:T(8,128)(2,1)}, bf16[2048,1024]{1,0:T(8,128)(2,1)}, bf16[2048,1024]{1,0:T(8,128)(2,1)}, bf16[2048,1408]{1,0:T(8,128)(2,1)}, bf...) custom-call(s32[19]{0:T(128)S(1)} %pad_add_fusion.meta, ...), custom_call_target="tpu_custom_call", output_to_operand_aliasing={{0}: (19, {}), {1}: (20, {}), {2}: (21, {}), {3}: (22, {}),... | custom-call | flops 5502926848 | bytes 1000 | tf_op jit(solution)/shard_map/experts/pallas_call | solution.py:727
  175.0 10.8 %experts.8 = (bf16[2048,1024]{1,0:T(8,128)(2,1)}, bf16[2048,1024]{1,0:T(8,128)(2,1)}, bf16[2048,1024]{1,0:T(8,128)(2,1)}, bf16[2048,1408]{1,0:T(8,128)(2,1)}, bf...) custom-call(s32[19]{0:T(128)S(1)} %pad_add_fusion.meta, ...), custom_call_target="tpu_custom_call", output_to_operand_aliasing={{0}: (19, {}), {1}: (20, {}), {2}: (21, {}), {3}: (22, {}),... | custom-call | flops 5502926848 | bytes 1000 | tf_op jit(solution)/shard_map/experts/pallas_call | solution.py:727
  189.5 10.5 %experts.9 = (bf16[2048,1024]{1,0:T(8,128)(2,1)}, bf16[2048,1024]{1,0:T(8,128)(2,1)}, bf16[2048,1024]{1,0:T(8,128)(2,1)}, bf16[2048,1408]{1,0:T(8,128)(2,1)}, bf...) custom-call(s32[19]{0:T(128)S(1)} %pad_add_fusion.meta, ...), custom_call_target="tpu_custom_call", output_to_operand_aliasing={{0}: (19, {}), {1}: (20, {}), {2}: (21, {}), {3}: (22, {}),... | custom-call | flops 5502926848 | bytes 1000 | tf_op jit(solution)/shard_map/experts/pallas_call | solution.py:727
  206.3 20.0 %experts.10 = (bf16[2048,1024]{1,0:T(8,128)(2,1)}, bf16[2048,1024]{1,0:T(8,128)(2,1)}, bf16[2048,1024]{1,0:T(8,128)(2,1)}, bf16[2048,1408]{1,0:T(8,128)(2,1)}, b...) custom-call(s32[19]{0:T(128)S(1)} %pad_add_fusion.meta, ...), custom_call_target="tpu_custom_call", output_to_operand_aliasing={{0}: (19, {}), {1}: (20, {}), {2}: (21, {}), {3}: (22, {}),... | custom-call | flops 11005853696 | bytes 1000 | tf_op jit(solution)/shard_map/experts/pallas_call | solution.py:727
  229.4 19.6 %experts.11 = (bf16[2048,1024]{1,0:T(8,128)(2,1)}, bf16[2048,1024]{1,0:T(8,128)(2,1)}, bf16[2048,1024]{1,0:T(8,128)(2,1)}, bf16[2048,1408]{1,0:T(8,128)(2,1)}, b...) custom-call(s32[19]{0:T(128)S(1)} %pad_add_fusion.meta, ...), custom_call_target="tpu_custom_call", output_to_operand_aliasing={{0}: (19, {}), {1}: (20, {}), {2}: (21, {}), {3}: (22, {}),... | custom-call | flops 11005853696 | bytes 1000 | tf_op jit(solution)/shard_map/experts/pallas_call | solution.py:727
  260.5 6.6 %convolution_convert_fusion.2 = bf16[1408,1024]{1,0:T(8,128)(2,1)S(1)} fusion(bf16[2048,1408]{1,0:T(8,128)(2,1)S(1)} %bitcast.204, bf16[2048,1024]{1,0:T(8,128)(2,1)S(1)} %copy-done.102), kind=kOutput, calls=%fused_computation.8 | convolution fusion | flops 5907021824 | bytes 12845056 | tf_op jit(solution)/shard_map/dot_general | solution.py:23
  268.4 8.8 %collective-permute-start.42 = (bf16[704,1024]{1,0:T(8,128)(2,1)}, bf16[704,1024]{1,0:T(8,128)(2,1)}, u32[]{:S(2)}, u32[]{:S(2)}) collective-permute-start(bf16[704,1024]{1,0:T(8,128)(2,1)} %dynamic-slice_bitcast_fusion.2), channel_id=1, source_target_pairs={{0,1},{1,0},{2,3},{3,2},{4,5},{5,4},{6,7},{7,6},{8,9},{9,8},{10,11... | collective-permute-start | bytes 4325384 | tf_op jit(solution)/shard_map/ppermute | solution.py:176
  278.9 4.8 convolution_convert_fusion.3
  289.1 6.4 %convolution_convert_fusion.1 = bf16[1408,1024]{1,0:T(8,128)(2,1)S(1)} fusion(bf16[2048,1408]{1,0:T(8,128)(2,1)S(1)} %bitcast.206, bf16[2048,1024]{1,0:T(8,128)(2,1)S(1)} %copy-done.101), kind=kOutput, calls=%fused_computation.7 | convolution fusion | flops 5907021824 | bytes 12845056 | tf_op jit(solution)/shard_map/dot_general | solution.py:23
  299.7 5.8 %attend_back.4 = (bf16[3,1024,64]{2,1,0:T(8,128)(2,1)S(1)}, f32[8,2048]{1,0:T(8,128)S(1)}) custom-call(s32[19]{0:T(128)S(1)} %pad_add_fusion.meta, bf16[6,1024,64]{2,1,0:T(8,128)(2,1)S(1)} %copy-done.98, bf16[6,1024,64]{2,1,0:T(8,128)(2,1)S(1)} %copy-done.98, bf16[6,1024,64]{2,1,0:T(8,128)(2,1)S(1)} %copy-done.98, bf16[8,256,1024]{2,1,0:T(8,128)(2,1)S(1)} %copy-done.4, ...), custom_call_target="tpu_custom_call" | custom-call | flops 6000000000 | bytes 1000 | tf_op jit(solution)/shard_map/attend_back/pallas_call | solution.py:844
  313.5 5.8 %attend_back.5 = (bf16[3,1024,64]{2,1,0:T(8,128)(2,1)S(1)}, f32[8,2048]{1,0:T(8,128)S(1)}) custom-call(s32[19]{0:T(128)S(1)} %pad_add_fusion.meta, bf16[6,1024,64]{2,1,0:T(8,128)(2,1)S(1)} %copy-done.98, bf16[6,1024,64]{2,1,0:T(8,128)(2,1)S(1)} %copy-done.98, bf16[6,1024,64]{2,1,0:T(8,128)(2,1)S(1)} %copy-done.98, bf16[8,256,1024]{2,1,0:T(8,128)(2,1)S(1)} %copy-done.4, ...), custom_call_target="tpu_custom_call" | custom-call | flops 6000000000 | bytes 1000 | tf_op jit(solution)/shard_map/attend_back/pallas_call | solution.py:844
  331.3 8.4 %collective-permute-done.51.got = bf16[704,1024]{1,0:T(8,128)(2,1)} collective-permute-done((bf16[704,1024]{1,0:T(8,128)(2,1)}, bf16[704,1024]{1,0:T(8,128)(2,1)}, u32[]{:S(2)}, u32[]{:S(2)}) %collective-permute-start.51) | collective-permute-done | bytes 1441824 | tf_op jit(solution)/shard_map/ppermute | solution.py:176
  339.7 6.4 %convolution_convert_fusion = bf16[1408,1024]{1,0:T(8,128)(2,1)S(1)} fusion(bf16[2048,1408]{1,0:T(8,128)(2,1)S(1)} %bitcast.208, bf16[2048,1024]{1,0:T(8,128)(2,1)S(1)} %copy-done.101), kind=kOutput, calls=%fused_computation.6 | convolution fusion | flops 5907021824 | bytes 12845056 | tf_op jit(solution)/shard_map/dot_general | solution.py:23
  351.4 6.1 %collective-permute-done.50.left = bf16[104,1024]{1,0:T(8,128)(2,1)S(1)} collective-permute-done((bf16[104,1024]{1,0:T(8,128)(2,1)S(1)}, bf16[104,1024]{1,0:T(8,128)(2,1)S(1)}, u32[]{:S(2)}, u32[]{:S(2)}) %collective-permute-start.50) | collective-permute-done | bytes 213024 | tf_op jit(solution)/shard_map/ppermute | solution.py:41
  359.3 5.8 %attend_back.6 = (bf16[3,1024,64]{2,1,0:T(8,128)(2,1)S(1)}, f32[8,2048]{1,0:T(8,128)S(1)}) custom-call(s32[19]{0:T(128)S(1)} %pad_add_fusion.meta, bf16[6,1024,64]{2,1,0:T(8,128)(2,1)S(1)} %copy-done.96, bf16[6,1024,64]{2,1,0:T(8,128)(2,1)S(1)} %copy-done.96, bf16[6,1024,64]{2,1,0:T(8,128)(2,1)S(1)} %copy-done.96, bf16[8,256,1024]{2,1,0:T(8,128)(2,1)S(1)} %copy-done.5, ...), custom_call_target="tpu_custom_call" | custom-call | flops 6000000000 | bytes 1000 | tf_op jit(solution)/shard_map/attend_back/pallas_call | solution.py:844
  371.6 11.5 %collective-permute-done.55.got = bf16[704,1024]{1,0:T(8,128)(2,1)} collective-permute-done((bf16[704,1024]{1,0:T(8,128)(2,1)}, bf16[704,1024]{1,0:T(8,128)(2,1)}, u32[]{:S(2)}, u32[]{:S(2)}) %collective-permute-start.55) | collective-permute-done | bytes 1441824 | tf_op jit(solution)/shard_map/ppermute | solution.py:176
  384.7 5.8 %attend_back.7 = (bf16[3,1024,64]{2,1,0:T(8,128)(2,1)S(1)}, f32[8,2048]{1,0:T(8,128)S(1)}) custom-call(s32[19]{0:T(128)S(1)} %pad_add_fusion.meta, bf16[6,1024,64]{2,1,0:T(8,128)(2,1)S(1)} %copy-done.96, bf16[6,1024,64]{2,1,0:T(8,128)(2,1)S(1)} %copy-done.96, bf16[6,1024,64]{2,1,0:T(8,128)(2,1)S(1)} %copy-done.96, bf16[8,256,1024]{2,1,0:T(8,128)(2,1)S(1)} %copy-done.5, ...), custom_call_target="tpu_custom_call" | custom-call | flops 6000000000 | bytes 1000 | tf_op jit(solution)/shard_map/attend_back/pallas_call | solution.py:844
  438.8 4.0 all-to-all-start.1
  453.7 4.8 widen.5
  458.6 4.8 widen.3
  482.9 4.8 widen.4
  (556 shorter events, 234.4 us)
Async XLA Ops:
  40.4 21.2 %collective-permute-start.8 = (bf16[8,32,384]{2,1,0:T(8,128)(2,1)S(1)}, bf16[8,32,384]{2,1,0:T(8,128)(2,1)S(1)}, u32[]{:S(2)}, u32[]{:S(2)}) collective-permute-start(bf16[8,32,384]{2,1,0:T(8,128)(2,1)S(1)} %all-to-all-done.refs_0_), channel_id=1, source_target_pairs={{0,2},{1,3},{2,0},{3,1},{4,6},{5,7},{6,4},{7,5},{8,10},{9,11},{10,... | collective-permute-start | bytes 589832 | tf_op jit(solution)/shard_map/ppermute | solution.py:176
  105.7 16.8 %collective-permute-start.20 = (bf16[8,32,1024]{2,1,0:T(8,128)(2,1)}, bf16[8,32,1024]{2,1,0:T(8,128)(2,1)}, u32[]{:S(2)}, u32[]{:S(2)}) collective-permute-start(bf16[8,32,1024]{2,1,0:T(8,128)(2,1)} %slice.201.refs_0_), channel_id=1, source_target_pairs={{0,1},{1,0},{2,3},{3,2},{4,5},{5,4},{6,7},{7,6},{8,9},{9,8},{10,11... | collective-permute-start | bytes 1572872 | tf_op jit(solution)/shard_map/ppermute | solution.py:176
  120.3 25.3 %collective-permute-start.22 = (bf16[256,1024]{1,0:T(8,128)(2,1)}, bf16[256,1024]{1,0:T(8,128)(2,1)}, u32[]{:S(2)}, u32[]{:S(2)}) collective-permute-start(bf16[256,1024]{1,0:T(8,128)(2,1)} %copy-done.64), channel_id=1, source_target_pairs={{0,8},{8,16},{16,24},{24,28},{28,20},{20,12},{12,4},{4,0},{1,9},{9... | collective-permute-start | bytes 1572872 | tf_op jit(solution)/shard_map/ppermute | solution.py:41
  121.8 23.8 %collective-permute-start.23 = (bf16[256,1024]{1,0:T(8,128)(2,1)}, bf16[256,1024]{1,0:T(8,128)(2,1)}, u32[]{:S(2)}, u32[]{:S(2)}) collective-permute-start(bf16[256,1024]{1,0:T(8,128)(2,1)} %copy-done.64), channel_id=1, source_target_pairs={{0,4},{8,0},{16,8},{24,16},{28,24},{20,28},{12,20},{4,12},{1,5},{9... | collective-permute-start | bytes 1572872 | tf_op jit(solution)/shard_map/ppermute | solution.py:41
  157.8 28.1 %collective-permute-start.26 = (bf16[256,1024]{1,0:T(8,128)(2,1)}, bf16[256,1024]{1,0:T(8,128)(2,1)}, u32[]{:S(2)}, u32[]{:S(2)}) collective-permute-start(bf16[256,1024]{1,0:T(8,128)(2,1)} %collective-permute-done.24.refs_4_), channel_id=1, source_target_pairs={{0,8},{8,16},{16,24},{24,28},{28,20},{20,12},{12,4},{4,0},{1,9},{9... | collective-permute-start | bytes 1572872 | tf_op jit(solution)/shard_map/ppermute | solution.py:41
  159.2 26.7 %collective-permute-start.27 = (bf16[256,1024]{1,0:T(8,128)(2,1)}, bf16[256,1024]{1,0:T(8,128)(2,1)}, u32[]{:S(2)}, u32[]{:S(2)}) collective-permute-start(bf16[256,1024]{1,0:T(8,128)(2,1)} %collective-permute-done.25.refs_5_), channel_id=1, source_target_pairs={{0,4},{8,0},{16,8},{24,16},{28,24},{20,28},{12,20},{4,12},{1,5},{9... | collective-permute-start | bytes 1572872 | tf_op jit(solution)/shard_map/ppermute | solution.py:41
  201.1 25.1 %collective-permute-start.30 = (bf16[128,1024]{1,0:T(8,128)(2,1)S(1)}, bf16[128,1024]{1,0:T(8,128)(2,1)S(1)}, u32[]{:S(2)}, u32[]{:S(2)}) collective-permute-start(bf16[128,1024]{1,0:T(8,128)(2,1)S(1)} %get-tuple-element.267), channel_id=1, source_target_pairs={{0,8},{8,16},{16,24},{24,28},{28,20},{20,12},{12,4},{4,0},{1,9},{9... | collective-permute-start | bytes 786440 | tf_op jit(solution)/shard_map/ppermute | solution.py:41
  202.6 23.7 %collective-permute-start.31 = (bf16[128,1024]{1,0:T(8,128)(2,1)S(1)}, bf16[128,1024]{1,0:T(8,128)(2,1)S(1)}, u32[]{:S(2)}, u32[]{:S(2)}) collective-permute-start(bf16[128,1024]{1,0:T(8,128)(2,1)S(1)} %get-tuple-element.268), channel_id=1, source_target_pairs={{0,4},{8,0},{16,8},{24,16},{28,24},{20,28},{12,20},{4,12},{1,5},{9... | collective-permute-start | bytes 786440 | tf_op jit(solution)/shard_map/ppermute | solution.py:41
  227.4 27.1 %collective-permute-start.32 = (bf16[256,1024]{1,0:T(8,128)(2,1)}, bf16[256,1024]{1,0:T(8,128)(2,1)}, u32[]{:S(2)}, u32[]{:S(2)}) collective-permute-start(bf16[256,1024]{1,0:T(8,128)(2,1)} %get-tuple-element.282), channel_id=1, source_target_pairs={{0,8},{8,16},{16,24},{24,28},{28,20},{20,12},{12,4},{4,0},{1,9},{9... | collective-permute-start | bytes 1572872 | tf_op jit(solution)/shard_map/ppermute | solution.py:41
  228.8 25.7 %collective-permute-start.33 = (bf16[256,1024]{1,0:T(8,128)(2,1)}, bf16[256,1024]{1,0:T(8,128)(2,1)}, u32[]{:S(2)}, u32[]{:S(2)}) collective-permute-start(bf16[256,1024]{1,0:T(8,128)(2,1)} %get-tuple-element.283), channel_id=1, source_target_pairs={{0,4},{8,0},{16,8},{24,16},{28,24},{20,28},{12,20},{4,12},{1,5},{9... | collective-permute-start | bytes 1572872 | tf_op jit(solution)/shard_map/ppermute | solution.py:41
  258.3 18.9 %collective-permute-start.34 = (bf16[256,1024]{1,0:T(8,128)(2,1)S(1)}, bf16[256,1024]{1,0:T(8,128)(2,1)S(1)}, u32[]{:S(2)}, u32[]{:S(2)}) collective-permute-start(bf16[256,1024]{1,0:T(8,128)(2,1)S(1)} %get-tuple-element.297), channel_id=1, source_target_pairs={{0,8},{8,16},{16,24},{24,28},{28,20},{20,12},{12,4},{4,0},{1,9},{9... | collective-permute-start | bytes 1572872 | tf_op jit(solution)/shard_map/ppermute | solution.py:41
  259.8 17.5 %collective-permute-start.35 = (bf16[256,1024]{1,0:T(8,128)(2,1)S(1)}, bf16[256,1024]{1,0:T(8,128)(2,1)S(1)}, u32[]{:S(2)}, u32[]{:S(2)}) collective-permute-start(bf16[256,1024]{1,0:T(8,128)(2,1)S(1)} %get-tuple-element.298), channel_id=1, source_target_pairs={{0,4},{8,0},{16,8},{24,16},{28,24},{20,28},{12,20},{4,12},{1,5},{9... | collective-permute-start | bytes 1572872 | tf_op jit(solution)/shard_map/ppermute | solution.py:41
  268.4 37.2 %collective-permute-start.42 = (bf16[704,1024]{1,0:T(8,128)(2,1)}, bf16[704,1024]{1,0:T(8,128)(2,1)}, u32[]{:S(2)}, u32[]{:S(2)}) collective-permute-start(bf16[704,1024]{1,0:T(8,128)(2,1)} %dynamic-slice_bitcast_fusion.2), channel_id=1, source_target_pairs={{0,1},{1,0},{2,3},{3,2},{4,5},{5,4},{6,7},{7,6},{8,9},{9,8},{10,11... | collective-permute-start | bytes 4325384 | tf_op jit(solution)/shard_map/ppermute | solution.py:176
  278.9 17.8 %collective-permute-start.39 = (bf16[128,1024]{1,0:T(8,128)(2,1)S(1)}, bf16[128,1024]{1,0:T(8,128)(2,1)S(1)}, u32[]{:S(2)}, u32[]{:S(2)}) collective-permute-start(bf16[128,1024]{1,0:T(8,128)(2,1)S(1)} %get-tuple-element.308), channel_id=1, source_target_pairs={{0,4},{8,0},{16,8},{24,16},{28,24},{20,28},{12,20},{4,12},{1,5},{9... | collective-permute-start | bytes 786440 | tf_op jit(solution)/shard_map/ppermute | solution.py:41
  287.0 23.9 %collective-permute-start.43 = (bf16[8,80,1024]{2,1,0:T(8,128)(2,1)}, bf16[8,80,1024]{2,1,0:T(8,128)(2,1)S(1)}, u32[]{:S(2)}, u32[]{:S(2)}) collective-permute-start(bf16[8,80,1024]{2,1,0:T(8,128)(2,1)} %dynamic-slice_bitcast_fusion.3), channel_id=1, source_target_pairs={{0,1},{1,0},{2,3},{3,2},{4,5},{5,4},{6,7},{7,6},{8,9},{9,8},{10,11... | collective-permute-start | bytes 3932168 | tf_op jit(solution)/shard_map/ppermute | solution.py:176
  296.7 23.3 %collective-permute-start.46 = (bf16[704,1024]{1,0:T(8,128)(2,1)}, bf16[704,1024]{1,0:T(8,128)(2,1)}, u32[]{:S(2)}, u32[]{:S(2)}) collective-permute-start(bf16[704,1024]{1,0:T(8,128)(2,1)} %dynamic-slice_bitcast_fusion.1), channel_id=1, source_target_pairs={{0,1},{1,0},{2,3},{3,2},{4,5},{5,4},{6,7},{7,6},{8,9},{9,8},{10,11... | collective-permute-start | bytes 4325384 | tf_op jit(solution)/shard_map/ppermute | solution.py:176
  308.7 31.0 %collective-permute-start.51 = (bf16[704,1024]{1,0:T(8,128)(2,1)}, bf16[704,1024]{1,0:T(8,128)(2,1)}, u32[]{:S(2)}, u32[]{:S(2)}) collective-permute-start(bf16[704,1024]{1,0:T(8,128)(2,1)} %fusion.3.kept), channel_id=1, source_target_pairs={{0,2},{1,3},{2,0},{3,1},{4,6},{5,7},{6,4},{7,5},{8,10},{9,11},{10,... | collective-permute-start | bytes 4325384 | tf_op jit(solution)/shard_map/ppermute | solution.py:176
  328.6 29.0 %collective-permute-start.48 = (bf16[256,1024]{1,0:T(8,128)(2,1)S(1)}, bf16[256,1024]{1,0:T(8,128)(2,1)S(1)}, u32[]{:S(2)}, u32[]{:S(2)}) collective-permute-start(bf16[256,1024]{1,0:T(8,128)(2,1)S(1)} %get-tuple-element.335), channel_id=1, source_target_pairs={{0,4},{8,0},{16,8},{24,16},{28,24},{20,28},{12,20},{4,12},{1,5},{9... | collective-permute-start | bytes 1572872 | tf_op jit(solution)/shard_map/ppermute | solution.py:41
  329.8 27.9 %collective-permute-start.47 = (bf16[256,1024]{1,0:T(8,128)(2,1)S(1)}, bf16[256,1024]{1,0:T(8,128)(2,1)S(1)}, u32[]{:S(2)}, u32[]{:S(2)}) collective-permute-start(bf16[256,1024]{1,0:T(8,128)(2,1)S(1)} %get-tuple-element.334), channel_id=1, source_target_pairs={{0,8},{8,16},{16,24},{24,28},{28,20},{20,12},{12,4},{4,0},{1,9},{9... | collective-permute-start | bytes 1572872 | tf_op jit(solution)/shard_map/ppermute | solution.py:41
  330.9 20.0 %collective-permute-start.49 = (bf16[104,1024]{1,0:T(8,128)(2,1)S(1)}, bf16[104,1024]{1,0:T(8,128)(2,1)S(1)}, u32[]{:S(2)}, u32[]{:S(2)}) collective-permute-start(bf16[104,1024]{1,0:T(8,128)(2,1)S(1)} %slice_bitcast_fusion.11), channel_id=1, source_target_pairs={{0,8},{8,16},{16,24},{24,28},{28,20},{20,12},{12,4},{4,0},{1,9},{9... | collective-permute-start | bytes 638984 | tf_op jit(solution)/shard_map/ppermute | solution.py:41
  346.2 23.4 %collective-permute-start.54 = (bf16[704,1024]{1,0:T(8,128)(2,1)S(1)}, bf16[704,1024]{1,0:T(8,128)(2,1)S(1)}, u32[]{:S(2)}, u32[]{:S(2)}) collective-permute-start(bf16[704,1024]{1,0:T(8,128)(2,1)S(1)} %dynamic-slice_bitcast_fusion), channel_id=1, source_target_pairs={{0,1},{1,0},{2,3},{3,2},{4,5},{5,4},{6,7},{7,6},{8,9},{9,8},{10,11... | collective-permute-start | bytes 4325384 | tf_op jit(solution)/shard_map/ppermute | solution.py:176
  349.6 33.5 %collective-permute-start.55 = (bf16[704,1024]{1,0:T(8,128)(2,1)}, bf16[704,1024]{1,0:T(8,128)(2,1)}, u32[]{:S(2)}, u32[]{:S(2)}) collective-permute-start(bf16[704,1024]{1,0:T(8,128)(2,1)} %fusion.2.kept), channel_id=1, source_target_pairs={{0,2},{1,3},{2,0},{3,1},{4,6},{5,7},{6,4},{7,5},{8,10},{9,11},{10,... | collective-permute-start | bytes 4325384 | tf_op jit(solution)/shard_map/ppermute | solution.py:176
  371.4 54.2 %collective-permute-start.69 = (bf16[704,1024]{1,0:T(8,128)(2,1)}, bf16[704,1024]{1,0:T(8,128)(2,1)}, u32[]{:S(2)}, u32[]{:S(2)}) collective-permute-start(bf16[704,1024]{1,0:T(8,128)(2,1)} %fusion.1.kept), channel_id=1, source_target_pairs={{0,2},{1,3},{2,0},{3,1},{4,6},{5,7},{6,4},{7,5},{8,10},{9,11},{10,... | collective-permute-start | bytes 4325384 | tf_op jit(solution)/shard_map/ppermute | solution.py:176
  418.2 27.4 %collective-permute-start.80 = (bf16[704,1024]{1,0:T(8,128)(2,1)}, bf16[704,1024]{1,0:T(8,128)(2,1)}, u32[]{:S(2)}, u32[]{:S(2)}) collective-permute-start(bf16[704,1024]{1,0:T(8,128)(2,1)} %fusion.3.kept), channel_id=1, source_target_pairs={{0,1},{1,0},{2,3},{3,2},{4,5},{5,4},{6,7},{7,6},{8,9},{9,8},{10,11... | collective-permute-start | bytes 4325384 | tf_op jit(solution)/shard_map/ppermute | solution.py:176
  421.6 28.6 %collective-permute-start.81 = (bf16[704,1024]{1,0:T(8,128)(2,1)}, bf16[704,1024]{1,0:T(8,128)(2,1)}, u32[]{:S(2)}, u32[]{:S(2)}) collective-permute-start(bf16[704,1024]{1,0:T(8,128)(2,1)} %collective-permute-done.51.got), channel_id=1, source_target_pairs={{0,1},{1,0},{2,3},{3,2},{4,5},{5,4},{6,7},{7,6},{8,9},{9,8},{10,11... | collective-permute-start | bytes 4325384 | tf_op jit(solution)/shard_map/ppermute | solution.py:176
  429.0 29.4 %collective-permute-start.76 = (bf16[704,1024]{1,0:T(8,128)(2,1)}, bf16[704,1024]{1,0:T(8,128)(2,1)}, u32[]{:S(2)}, u32[]{:S(2)}) collective-permute-start(bf16[704,1024]{1,0:T(8,128)(2,1)} %fusion.2.kept), channel_id=1, source_target_pairs={{0,1},{1,0},{2,3},{3,2},{4,5},{5,4},{6,7},{7,6},{8,9},{9,8},{10,11... | collective-permute-start | bytes 4325384 | tf_op jit(solution)/shard_map/ppermute | solution.py:176
  431.3 27.3 %collective-permute-start.77 = (bf16[704,1024]{1,0:T(8,128)(2,1)}, bf16[704,1024]{1,0:T(8,128)(2,1)}, u32[]{:S(2)}, u32[]{:S(2)}) collective-permute-start(bf16[704,1024]{1,0:T(8,128)(2,1)} %collective-permute-done.55.got), channel_id=1, source_target_pairs={{0,1},{1,0},{2,3},{3,2},{4,5},{5,4},{6,7},{7,6},{8,9},{9,8},{10,11... | collective-permute-start | bytes 4325384 | tf_op jit(solution)/shard_map/ppermute | solution.py:176
  438.8 27.4 %all-to-all-start.1 = ((bf16[8,48,384]{2,1,0:T(8,128)(2,1)}), bf16[8,48,384]{2,1,0:T(8,128)(2,1)S(1)}, u32[]{:S(2)}, u32[]{:S(2)}) async-start(bf16[8,48,384]{2,1,0:T(8,128)(2,1)} %fusion.23), calls=%async_computation.1 | async-start | bytes 589824 | tf_op jit(solution)/shard_map/all_to_all | solution.py:1252
  445.5 18.4 %collective-permute-start.64 = (bf16[128,1024]{1,0:T(8,128)(2,1)S(1)}, bf16[128,1024]{1,0:T(8,128)(2,1)S(1)}, u32[]{:S(2)}, u32[]{:S(2)}) collective-permute-start(bf16[128,1024]{1,0:T(8,128)(2,1)S(1)} %get-tuple-element.367), channel_id=1, source_target_pairs={{0,8},{8,16},{16,24},{24,28},{28,20},{20,12},{12,4},{4,0},{1,9},{9... | collective-permute-start | bytes 786440 | tf_op jit(solution)/shard_map/ppermute | solution.py:41
  447.6 16.3 %collective-permute-start.65 = (bf16[128,1024]{1,0:T(8,128)(2,1)S(1)}, bf16[128,1024]{1,0:T(8,128)(2,1)S(1)}, u32[]{:S(2)}, u32[]{:S(2)}) collective-permute-start(bf16[128,1024]{1,0:T(8,128)(2,1)S(1)} %get-tuple-element.368), channel_id=1, source_target_pairs={{0,4},{8,0},{16,8},{24,16},{28,24},{20,28},{12,20},{4,12},{1,5},{9... | collective-permute-start | bytes 786440 | tf_op jit(solution)/shard_map/ppermute | solution.py:41
  458.5 24.4 %collective-permute-start.78 = (bf16[704,1024]{1,0:T(8,128)(2,1)}, bf16[704,1024]{1,0:T(8,128)(2,1)}, u32[]{:S(2)}, u32[]{:S(2)}) collective-permute-start(bf16[704,1024]{1,0:T(8,128)(2,1)} %fusion.1.kept), channel_id=1, source_target_pairs={{0,1},{1,0},{2,3},{3,2},{4,5},{5,4},{6,7},{7,6},{8,9},{9,8},{10,11... | collective-permute-start | bytes 4325384 | tf_op jit(solution)/shard_map/ppermute | solution.py:176
  463.4 19.5 %collective-permute-start.79 = (bf16[704,1024]{1,0:T(8,128)(2,1)}, bf16[704,1024]{1,0:T(8,128)(2,1)}, u32[]{:S(2)}, u32[]{:S(2)}) collective-permute-start(bf16[704,1024]{1,0:T(8,128)(2,1)} %collective-permute-done.69.got), channel_id=1, source_target_pairs={{0,1},{1,0},{2,3},{3,2},{4,5},{5,4},{6,7},{7,6},{8,9},{9,8},{10,11... | collective-permute-start | bytes 4325384 | tf_op jit(solution)/shard_map/ppermute | solution.py:176
  (175 other events, 1739.1 us)
where the time goes:
time: 497 us; the launch traced here: 488 us
  Pallas kernels  157 us (32%)
  starting transfers between devices  107 us (22%)
  waiting for transfers between devices  85.3 us (17%)
  local copies, waits for them, and re-layouts  80.1 us (16%)
  matrix products  32.5 us (7%)
  other arithmetic  23.1 us (5%)
    pallas_call x6, Pallas kernels, experts(): pl.pallas_call(functools.partial(experts_kernel, static), out_shape=[low(...  82.1 us
    ppermute x56, waiting for transfers between devices, ring_send(): return lax.ppermute(value, 'shard', pairs)  62.5 us
    unnamed x258, local copies, waits for them, and re-layouts  54.6 us
    ppermute x26, starting transfers between devices, swap(): return lax.ppermute(value, axis, [(i, i ^ bit) for i in range(count)])  49.7 us
    ppermute x56, starting transfers between devices, ring_send(): return lax.ppermute(value, 'shard', pairs)  49 us
    dot_general x7, matrix products, dot_tn(): lax.dot_general(left, right, (((0,), (0,)), ((), ())), preferred_element_...  31.8 us
    pallas_call x4, Pallas kernels, attend_back(): pl.pallas_call(functools.partial(attend_back_kernel, seq, head, heads), o...  23.3 us
    ppermute x26, waiting for transfers between devices, swap(): return lax.ppermute(value, axis, [(i, i ^ bit) for i in range(count)])  22.7 us
  transfers between devices with their start and end apart: 84, of which 27 were waited for; matrix products, arithmetic and copies ran while one was open for 16% of the time, Pallas kernels for 29%

commit v1 on v0

--- a/solution.py
+++ b/solution.py
@@ -156,9 +156,10 @@
     def last(self):
         return (self.right, self.left)
 
-    def total(self):
-        total = self.chunk(0).astype(f32)
-        return total + self.right.astype(f32) + self.left.astype(f32)
+
+def total_of(ring):
+    total = ring.chunk(0).astype(f32)
+    return total + ring.right.astype(f32) + ring.left.astype(f32)
 
 
 def fire(rings, *waits):
@@ -1195,7 +1196,8 @@
     rings = [second, final[0]]
     step(rings, waits)
     done = total_grad(grad_up, normed, (waits, totals[0].got))
-    waits = (done, sent(rings))
+    wide = totals[0].finish()
+    waits = (done, wide, sent(rings))
     while not second.done:
         step(rings, waits)
         waits = lasts(rings)
@@ -1207,9 +1209,9 @@
         waits = (parts[-1], sent(rings))
         if head == 0:
             totals[2].cross()
-            waits = waits + (totals[2].kept, totals[1].got)
+            waits = waits + (totals[2].kept,)
     step(rings, waits)
-    grads_last = back_norm(1, parts, waits)
+    grads_last = back_norm(1, parts, (waits, totals[1].got))
     final.append(Sum([(grads_last, 0, span)], count))
     waits = (grads_last, sent(rings))
     rings = final
@@ -1218,7 +1220,7 @@
         waits = lasts(rings)
 
     mix_first, mix_last, final_first, final_last = (
-        ring.total() for ring in (*sum_rings, *final)
+        total_of(ring) for ring in (*sum_rings, *final)
     )
     grad_tokens = jnp.stack([final_first[:span], final_last])
     positions = me * span + jnp.arange(span, dtype=jnp.int32)
@@ -1260,7 +1262,8 @@
     total_bias = total_bias.reshape(heads, bucket_count).T
 
     total_down, total_gate, total_up = (
-        total.finish().reshape(expert_count, unit_count, width) for total in totals
+        total.reshape(expert_count, unit_count, width)
+        for total in (wide, totals[1].finish(), totals[2].finish())
     )
     return (
         block_out,

time: 497 us -> 494 us (level)
  waiting for transfers between devices: 85.3 us -> 77.6 us
  local copies, waits for them, and re-layouts: 80.1 us -> 87.7 us
  starting transfers between devices: 107 us -> 101 us
    ppermute x26, waiting for transfers between devices: 22.7 us -> 9.33 us  [swap(): return lax.ppermute(value, axis, [(i, i ^ bit) for i in range(count)])]
    unnamed x258 -> x280, local copies, waits for them, and re-layouts: 54.6 us -> 61.5 us
    ppermute x56, waiting for transfers between devices: 62.5 us -> 68.2 us  [ring_send(): return lax.ppermute(value, 'shard', pairs)]
  transfers between devices with their start and end apart: 84 -> 84, of which waited for: 27 -> 27; matrix products, arithmetic and copies ran while one was open for 16% -> 17% of each run, Pallas kernels for 29% -> 30%
where the time goes in v1:
time: 494 us; the launch traced here: 484 us
  Pallas kernels  159 us (32%)
  starting transfers between devices  101 us (20%)
  local copies, waits for them, and re-layouts  87.7 us (18%)
  waiting for transfers between devices  77.6 us (16%)
  matrix products  32.5 us (7%)
  other arithmetic  23.8 us (5%)
    pallas_call x6, Pallas kernels, experts(): pl.pallas_call(functools.partial(experts_kernel, static), out_shape=[low(...  82 us
    ppermute x56, waiting for transfers between devices, ring_send(): return lax.ppermute(value, 'shard', pairs)  68.2 us
    unnamed x280, local copies, waits for them, and re-layouts  61.5 us
    ppermute x56, starting transfers between devices, ring_send(): return lax.ppermute(value, 'shard', pairs)  47.1 us
    ppermute x26, starting transfers between devices, swap(): return lax.ppermute(value, axis, [(i, i ^ bit) for i in range(count)])  45.1 us
    dot_general x7, matrix products, dot_tn(): lax.dot_general(left, right, (((0,), (0,)), ((), ())), preferred_element_...  31.8 us
    pallas_call x4, Pallas kernels, attend_back(): pl.pallas_call(functools.partial(attend_back_kernel, seq, head, heads), o...  25.3 us
    pallas_call x2, Pallas kernels, attend(): pl.pallas_call(functools.partial(attend_kernel, seq, seqs, places, heads,...  15.7 us
  transfers between devices with their start and end apart: 84, of which 27 were waited for; matrix products, arithmetic and copies ran while one was open for 17% of the time, Pallas kernels for 30%

profile of v1, /device:TPU:1, one launch (start us, length us, event | category | flops | bytes accessed | tf_op | source)
XLA Modules:
  0.0 484.5 jit_solution(9370064793854723627)
XLA Ops:
  7.4 13.7 %collective-permute-done.refs_1_ = bf16[304,1024]{1,0:T(8,128)(2,1)S(1)} collective-permute-done((bf16[304,1024]{1,0:T(8,128)(2,1)S(1)}, bf16[304,1024]{1,0:T(8,128)(2,1)S(1)}, u32[]{:S(2)}, u32[]{:S(2)}) %collective-permute-start) | collective-permute-done | bytes 622624 | tf_op jit(solution)/shard_map/ppermute | solution.py:41
  26.3 4.6 all-to-all-start
  30.9 4.9 %collective-permute-done.2.refs_3_ = bf16[304,1024]{1,0:T(8,128)(2,1)S(1)} collective-permute-done((bf16[304,1024]{1,0:T(8,128)(2,1)S(1)}, bf16[304,1024]{1,0:T(8,128)(2,1)S(1)}, u32[]{:S(2)}, u32[]{:S(2)}) %collective-permute-start.2) | collective-permute-done | bytes 622624 | tf_op jit(solution)/shard_map/ppermute | solution.py:41
  41.7 7.8 %collective-permute-done.4.refs_5_ = bf16[304,1024]{1,0:T(8,128)(2,1)S(1)} collective-permute-done((bf16[304,1024]{1,0:T(8,128)(2,1)S(1)}, bf16[304,1024]{1,0:T(8,128)(2,1)S(1)}, u32[]{:S(2)}, u32[]{:S(2)}) %collective-permute-start.4) | collective-permute-done | bytes 622624 | tf_op jit(solution)/shard_map/ppermute | solution.py:41
  50.9 4.0 collective-permute-start.6
  57.6 4.0 collective-permute-start.9
  66.2 8.1 %attend.2 = (bf16[1024,1024]{1,0:T(8,128)(2,1)S(1)}, bf16[6,1024,64]{2,1,0:T(8,128)(2,1)S(1)}, bf16[256,1024]{1,0:T(8,128)(2,1)S(1)}, bf16[8,48,1024]{2,1,0:T(8,128)(2,1)S(1)}) custom-call(s32[19]{0:T(128)S(1)} %pad_add_fusion.meta, bf16[304,1024]{1,0:T(8,128)(2,1)S(1)} %concatenate.44.refs_0_, bf16[304,1024]{1,0:T(8,128)(2,1)S(1)} %copy-done.95, ...), custom_call_target="tpu_custom_call" | custom-call | flops 8000000000 | bytes 1000 | tf_op jit(solution)/shard_map/attend/pallas_call | solution.py:431
  78.8 7.6 %attend.3 = (bf16[1024,1024]{1,0:T(8,128)(2,1)S(1)}, bf16[6,1024,64]{2,1,0:T(8,128)(2,1)S(1)}, bf16[256,1024]{1,0:T(8,128)(2,1)S(1)}) custom-call(s32[19]{0:T(128)S(1)} %pad_add_fusion.meta, bf16[304,1024]{1,0:T(8,128)(2,1)S(1)} %concatenate.44.refs_0_, bf16[304,1024]{1,0:T(8,128)(2,1)S(1)} %copy-done.95, bf16[304,1024]{1,0:T(8,128)(2,1)S(1)} %copy-done.97, ...), custom_call_target="tpu_custom_call" | custom-call | flops 8000000000 | bytes 1000 | tf_op jit(solution)/shard_map/attend/pallas_call | solution.py:431
  95.2 8.4 %collective-permute-done.13.refs_4_ = bf16[256,1024]{1,0:T(8,128)(2,1)S(1)} collective-permute-done((bf16[256,1024]{1,0:T(8,128)(2,1)S(1)}, bf16[256,1024]{1,0:T(8,128)(2,1)S(1)}, u32[]{:S(2)}, u32[]{:S(2)}) %collective-permute-start.13) | collective-permute-done | bytes 524320 | tf_op jit(solution)/shard_map/ppermute | solution.py:41
  109.0 5.6 %collective-permute-done.15.refs_6_ = bf16[256,1024]{1,0:T(8,128)(2,1)S(1)} collective-permute-done((bf16[256,1024]{1,0:T(8,128)(2,1)S(1)}, bf16[256,1024]{1,0:T(8,128)(2,1)S(1)}, u32[]{:S(2)}, u32[]{:S(2)}) %collective-permute-start.15) | collective-permute-done | bytes 524320 | tf_op jit(solution)/shard_map/ppermute | solution.py:41
  135.1 10.6 %experts.6 = (bf16[2048,1024]{1,0:T(8,128)(2,1)}, bf16[2048,1024]{1,0:T(8,128)(2,1)}, bf16[2048,1024]{1,0:T(8,128)(2,1)}, bf16[2048,1408]{1,0:T(8,128)(2,1)}, bf...) custom-call(s32[19]{0:T(128)S(1)} %pad_add_fusion.meta, ...), custom_call_target="tpu_custom_call" | custom-call | flops 5502926848 | bytes 1000 | tf_op jit(solution)/shard_map/experts/pallas_call | solution.py:728
  147.2 10.8 %experts.7 = (bf16[2048,1024]{1,0:T(8,128)(2,1)}, bf16[2048,1024]{1,0:T(8,128)(2,1)}, bf16[2048,1024]{1,0:T(8,128)(2,1)}, bf16[2048,1408]{1,0:T(8,128)(2,1)}, bf...) custom-call(s32[19]{0:T(128)S(1)} %pad_add_fusion.meta, ...), custom_call_target="tpu_custom_call", output_to_operand_aliasing={{0}: (19, {}), {1}: (20, {}), {2}: (21, {}), {3}: (22, {}),... | custom-call | flops 5502926848 | bytes 1000 | tf_op jit(solution)/shard_map/experts/pallas_call | solution.py:728
  174.5 10.5 %experts.8 = (bf16[2048,1024]{1,0:T(8,128)(2,1)}, bf16[2048,1024]{1,0:T(8,128)(2,1)}, bf16[2048,1024]{1,0:T(8,128)(2,1)}, bf16[2048,1408]{1,0:T(8,128)(2,1)}, bf...) custom-call(s32[19]{0:T(128)S(1)} %pad_add_fusion.meta, ...), custom_call_target="tpu_custom_call", output_to_operand_aliasing={{0}: (19, {}), {1}: (20, {}), {2}: (21, {}), {3}: (22, {}),... | custom-call | flops 5502926848 | bytes 1000 | tf_op jit(solution)/shard_map/experts/pallas_call | solution.py:728
  188.7 10.6 %experts.9 = (bf16[2048,1024]{1,0:T(8,128)(2,1)}, bf16[2048,1024]{1,0:T(8,128)(2,1)}, bf16[2048,1024]{1,0:T(8,128)(2,1)}, bf16[2048,1408]{1,0:T(8,128)(2,1)}, bf...) custom-call(s32[19]{0:T(128)S(1)} %pad_add_fusion.meta, ...), custom_call_target="tpu_custom_call", output_to_operand_aliasing={{0}: (19, {}), {1}: (20, {}), {2}: (21, {}), {3}: (22, {}),... | custom-call | flops 5502926848 | bytes 1000 | tf_op jit(solution)/shard_map/experts/pallas_call | solution.py:728
  205.5 20.0 %experts.10 = (bf16[2048,1024]{1,0:T(8,128)(2,1)}, bf16[2048,1024]{1,0:T(8,128)(2,1)}, bf16[2048,1024]{1,0:T(8,128)(2,1)}, bf16[2048,1408]{1,0:T(8,128)(2,1)}, b...) custom-call(s32[19]{0:T(128)S(1)} %pad_add_fusion.meta, ...), custom_call_target="tpu_custom_call", output_to_operand_aliasing={{0}: (19, {}), {1}: (20, {}), {2}: (21, {}), {3}: (22, {}),... | custom-call | flops 11005853696 | bytes 1000 | tf_op jit(solution)/shard_map/experts/pallas_call | solution.py:728
  228.6 19.6 %experts.11 = (bf16[2048,1024]{1,0:T(8,128)(2,1)}, bf16[2048,1024]{1,0:T(8,128)(2,1)}, bf16[2048,1024]{1,0:T(8,128)(2,1)}, bf16[2048,1408]{1,0:T(8,128)(2,1)}, b...) custom-call(s32[19]{0:T(128)S(1)} %pad_add_fusion.meta, ...), custom_call_target="tpu_custom_call", output_to_operand_aliasing={{0}: (19, {}), {1}: (20, {}), {2}: (21, {}), {3}: (22, {}),... | custom-call | flops 11005853696 | bytes 1000 | tf_op jit(solution)/shard_map/experts/pallas_call | solution.py:728
  259.8 6.6 %convolution_convert_fusion.2 = bf16[1408,1024]{1,0:T(8,128)(2,1)S(1)} fusion(bf16[2048,1408]{1,0:T(8,128)(2,1)S(1)} %bitcast.204, bf16[2048,1024]{1,0:T(8,128)(2,1)S(1)} %copy-done.107), kind=kOutput, calls=%fused_computation.8 | convolution fusion | flops 5907021824 | bytes 12845056 | tf_op jit(solution)/shard_map/dot_general | solution.py:23
  267.6 8.8 %collective-permute-start.42 = (bf16[704,1024]{1,0:T(8,128)(2,1)}, bf16[704,1024]{1,0:T(8,128)(2,1)S(1)}, u32[]{:S(2)}, u32[]{:S(2)}) collective-permute-start(bf16[704,1024]{1,0:T(8,128)(2,1)} %dynamic-slice_bitcast_fusion.2), channel_id=1, source_target_pairs={{0,1},{1,0},{2,3},{3,2},{4,5},{5,4},{6,7},{7,6},{8,9},{9,8},{10,11... | collective-permute-start | bytes 4325384 | tf_op jit(solution)/shard_map/ppermute | solution.py:177
  278.1 4.8 convolution_convert_fusion.3
  288.2 6.4 %convolution_convert_fusion.1 = bf16[1408,1024]{1,0:T(8,128)(2,1)S(1)} fusion(bf16[2048,1408]{1,0:T(8,128)(2,1)S(1)} %bitcast.206, bf16[2048,1024]{1,0:T(8,128)(2,1)S(1)} %copy-done.106), kind=kOutput, calls=%fused_computation.7 | convolution fusion | flops 5907021824 | bytes 12845056 | tf_op jit(solution)/shard_map/dot_general | solution.py:23
  299.4 5.8 %attend_back.4 = (bf16[3,1024,64]{2,1,0:T(8,128)(2,1)S(1)}, f32[8,2048]{1,0:T(8,128)S(1)}) custom-call(s32[19]{0:T(128)S(1)} %pad_add_fusion.meta, bf16[6,1024,64]{2,1,0:T(8,128)(2,1)S(1)} %copy-done.103, bf16[6,1024,64]{2,1,0:T(8,128)(2,1)S(1)} %copy-done.103, bf16[6,1024,64]{2,1,0:T(8,128)(2,1)S(1)} %copy-done.103, bf16[8,256,1024]{2,1,0:T(8,128)(2,1)S(1)} %copy-done.4, ...), custom_call_target="tpu_custom_call" | custom-call | flops 6000000000 | bytes 1000 | tf_op jit(solution)/shard_map/attend_back/pallas_call | solution.py:845
  315.8 5.8 %attend_back.5 = (bf16[3,1024,64]{2,1,0:T(8,128)(2,1)S(1)}, f32[8,2048]{1,0:T(8,128)S(1)}) custom-call(s32[19]{0:T(128)S(1)} %pad_add_fusion.meta, bf16[6,1024,64]{2,1,0:T(8,128)(2,1)S(1)} %copy-done.103, bf16[6,1024,64]{2,1,0:T(8,128)(2,1)S(1)} %copy-done.103, bf16[6,1024,64]{2,1,0:T(8,128)(2,1)S(1)} %copy-done.103, bf16[8,256,1024]{2,1,0:T(8,128)(2,1)S(1)} %copy-done.4, ...), custom_call_target="tpu_custom_call" | custom-call | flops 6000000000 | bytes 1000 | tf_op jit(solution)/shard_map/attend_back/pallas_call | solution.py:845
  331.5 7.0 %collective-permute-done.51.got = bf16[704,1024]{1,0:T(8,128)(2,1)} collective-permute-done((bf16[704,1024]{1,0:T(8,128)(2,1)}, bf16[704,1024]{1,0:T(8,128)(2,1)}, u32[]{:S(2)}, u32[]{:S(2)}) %collective-permute-start.51) | collective-permute-done | bytes 1441824 | tf_op jit(solution)/shard_map/ppermute | solution.py:177
  338.5 6.4 %convolution_convert_fusion = bf16[1408,1024]{1,0:T(8,128)(2,1)S(1)} fusion(bf16[2048,1408]{1,0:T(8,128)(2,1)S(1)} %bitcast.208, bf16[2048,1024]{1,0:T(8,128)(2,1)S(1)} %copy-done.106), kind=kOutput, calls=%fused_computation.6 | convolution fusion | flops 5907021824 | bytes 12845056 | tf_op jit(solution)/shard_map/dot_general | solution.py:23
  363.3 4.9 %widen.3 = f32[1408,1024]{1,0:T(8,128)} custom-call(s32[1]{0:T(128)} %bitcast.43.meta, bf16[704,1024]{1,0:T(8,128)(2,1)} %fusion.3.kept, bf16[704,1024]{1,0:T(8,128)(2,1)} %collective-permute-done.51.got, bf16[704,1024]{1,0:T(8,128)(2,1)} %collective-permute-done.52.kept_other, bf16[704,1024]{1,0:T(8,128)(2,1)} %collective-permute-done.53.got_other), custom_call_target="tpu_custom_call" | custom-call | tf_op jit(solution)/shard_map/widen/pallas_call | solution.py:283
  377.8 6.9 %attend_back.6 = (bf16[3,1024,64]{2,1,0:T(8,128)(2,1)S(1)}, f32[8,2048]{1,0:T(8,128)S(1)}) custom-call(s32[19]{0:T(128)S(1)} %pad_add_fusion.meta, bf16[6,1024,64]{2,1,0:T(8,128)(2,1)S(1)} %copy-done.101, bf16[6,1024,64]{2,1,0:T(8,128)(2,1)S(1)} %copy-done.101, bf16[6,1024,64]{2,1,0:T(8,128)(2,1)S(1)} %copy-done.101, bf16[8,256,1024]{2,1,0:T(8,128)(2,1)S(1)} %copy-done.7, ...), custom_call_target="tpu_custom_call" | custom-call | flops 6000000000 | bytes 1000 | tf_op jit(solution)/shard_map/attend_back/pallas_call | solution.py:845
  387.3 6.8 %attend_back.7 = (bf16[3,1024,64]{2,1,0:T(8,128)(2,1)S(1)}, f32[8,2048]{1,0:T(8,128)S(1)}) custom-call(s32[19]{0:T(128)S(1)} %pad_add_fusion.meta, bf16[6,1024,64]{2,1,0:T(8,128)(2,1)S(1)} %copy-done.101, bf16[6,1024,64]{2,1,0:T(8,128)(2,1)S(1)} %copy-done.101, bf16[6,1024,64]{2,1,0:T(8,128)(2,1)S(1)} %copy-done.101, bf16[8,256,1024]{2,1,0:T(8,128)(2,1)S(1)} %copy-done.7, ...), custom_call_target="tpu_custom_call" | custom-call | flops 6000000000 | bytes 1000 | tf_op jit(solution)/shard_map/attend_back/pallas_call | solution.py:845
  425.9 7.7 %collective-permute-done.59 = bf16[208,1024]{1,0:T(8,128)(2,1)S(1)} collective-permute-done((bf16[208,1024]{1,0:T(8,128)(2,1)S(1)}, bf16[208,1024]{1,0:T(8,128)(2,1)S(1)}, u32[]{:S(2)}, u32[]{:S(2)}) %collective-permute-start.59) | collective-permute-done | bytes 426016 | tf_op jit(solution)/shard_map/ppermute | solution.py:41
  441.3 4.1 all-to-all-start.1
  449.7 3.9 collective-permute-start.77
  454.6 4.8 widen.4
  479.2 4.8 widen.5
  (578 shorter events, 235.1 us)
Async XLA Ops:
  5.2 15.8 %collective-permute-start = (bf16[304,1024]{1,0:T(8,128)(2,1)S(1)}, bf16[304,1024]{1,0:T(8,128)(2,1)S(1)}, u32[]{:S(2)}, u32[]{:S(2)}) collective-permute-start(bf16[304,1024]{1,0:T(8,128)(2,1)S(1)} %concatenate.44.refs_0_), channel_id=1, source_target_pairs={{0,8},{8,16},{16,24},{24,28},{28,20},{20,12},{12,4},{4,0},{1,9},{9... | collective-permute-start | bytes 1867784 | tf_op jit(solution)/shard_map/ppermute | solution.py:41
  7.4 14.6 %collective-permute-start.1 = (bf16[304,1024]{1,0:T(8,128)(2,1)S(1)}, bf16[304,1024]{1,0:T(8,128)(2,1)S(1)}, u32[]{:S(2)}, u32[]{:S(2)}) collective-permute-start(bf16[304,1024]{1,0:T(8,128)(2,1)S(1)} %concatenate.44.refs_0_), channel_id=1, source_target_pairs={{0,4},{8,0},{16,8},{24,16},{28,24},{20,28},{12,20},{4,12},{1,5},{9... | collective-permute-start | bytes 1867784 | tf_op jit(solution)/shard_map/ppermute | solution.py:41
  40.4 21.2 %collective-permute-start.8 = (bf16[8,32,384]{2,1,0:T(8,128)(2,1)S(1)}, bf16[8,32,384]{2,1,0:T(8,128)(2,1)S(1)}, u32[]{:S(2)}, u32[]{:S(2)}) collective-permute-start(bf16[8,32,384]{2,1,0:T(8,128)(2,1)S(1)} %all-to-all-done.refs_0_), channel_id=1, source_target_pairs={{0,2},{1,3},{2,0},{3,1},{4,6},{5,7},{6,4},{7,5},{8,10},{9,11},{10,... | collective-permute-start | bytes 589832 | tf_op jit(solution)/shard_map/ppermute | solution.py:177
  94.0 15.0 %collective-permute-start.19 = (bf16[8,32,1024]{2,1,0:T(8,128)(2,1)}, bf16[8,32,1024]{2,1,0:T(8,128)(2,1)}, u32[]{:S(2)}, u32[]{:S(2)}) collective-permute-start(bf16[8,32,1024]{2,1,0:T(8,128)(2,1)} %slice.201.refs_0_), channel_id=1, source_target_pairs={{0,2},{1,3},{2,0},{3,1},{4,6},{5,7},{6,4},{7,5},{8,10},{9,11},{10,... | collective-permute-start | bytes 1572872 | tf_op jit(solution)/shard_map/ppermute | solution.py:177
  105.3 17.2 %collective-permute-start.20 = (bf16[8,32,1024]{2,1,0:T(8,128)(2,1)}, bf16[8,32,1024]{2,1,0:T(8,128)(2,1)}, u32[]{:S(2)}, u32[]{:S(2)}) collective-permute-start(bf16[8,32,1024]{2,1,0:T(8,128)(2,1)} %slice.201.refs_0_), channel_id=1, source_target_pairs={{0,1},{1,0},{2,3},{3,2},{4,5},{5,4},{6,7},{7,6},{8,9},{9,8},{10,11... | collective-permute-start | bytes 1572872 | tf_op jit(solution)/shard_map/ppermute | solution.py:177
  120.4 25.3 %collective-permute-start.22 = (bf16[256,1024]{1,0:T(8,128)(2,1)}, bf16[256,1024]{1,0:T(8,128)(2,1)}, u32[]{:S(2)}, u32[]{:S(2)}) collective-permute-start(bf16[256,1024]{1,0:T(8,128)(2,1)} %copy-done.69), channel_id=1, source_target_pairs={{0,8},{8,16},{16,24},{24,28},{28,20},{20,12},{12,4},{4,0},{1,9},{9... | collective-permute-start | bytes 1572872 | tf_op jit(solution)/shard_map/ppermute | solution.py:41
  121.7 24.0 %collective-permute-start.23 = (bf16[256,1024]{1,0:T(8,128)(2,1)}, bf16[256,1024]{1,0:T(8,128)(2,1)}, u32[]{:S(2)}, u32[]{:S(2)}) collective-permute-start(bf16[256,1024]{1,0:T(8,128)(2,1)} %copy-done.69), channel_id=1, source_target_pairs={{0,4},{8,0},{16,8},{24,16},{28,24},{20,28},{12,20},{4,12},{1,5},{9... | collective-permute-start | bytes 1572872 | tf_op jit(solution)/shard_map/ppermute | solution.py:41
  158.0 27.1 %collective-permute-start.26 = (bf16[256,1024]{1,0:T(8,128)(2,1)}, bf16[256,1024]{1,0:T(8,128)(2,1)}, u32[]{:S(2)}, u32[]{:S(2)}) collective-permute-start(bf16[256,1024]{1,0:T(8,128)(2,1)} %collective-permute-done.24.refs_4_), channel_id=1, source_target_pairs={{0,8},{8,16},{16,24},{24,28},{28,20},{20,12},{12,4},{4,0},{1,9},{9... | collective-permute-start | bytes 1572872 | tf_op jit(solution)/shard_map/ppermute | solution.py:41
  159.4 25.7 %collective-permute-start.27 = (bf16[256,1024]{1,0:T(8,128)(2,1)}, bf16[256,1024]{1,0:T(8,128)(2,1)}, u32[]{:S(2)}, u32[]{:S(2)}) collective-permute-start(bf16[256,1024]{1,0:T(8,128)(2,1)} %collective-permute-done.25.refs_5_), channel_id=1, source_target_pairs={{0,4},{8,0},{16,8},{24,16},{28,24},{20,28},{12,20},{4,12},{1,5},{9... | collective-permute-start | bytes 1572872 | tf_op jit(solution)/shard_map/ppermute | solution.py:41
  186.0 14.3 %collective-permute-start.28 = (bf16[128,1024]{1,0:T(8,128)(2,1)S(1)}, bf16[128,1024]{1,0:T(8,128)(2,1)S(1)}, u32[]{:S(2)}, u32[]{:S(2)}) collective-permute-start(bf16[128,1024]{1,0:T(8,128)(2,1)S(1)} %slice.207), channel_id=1, source_target_pairs={{0,8},{8,16},{16,24},{24,28},{28,20},{20,12},{12,4},{4,0},{1,9},{9... | collective-permute-start | bytes 786440 | tf_op jit(solution)/shard_map/ppermute | solution.py:41
  200.3 25.1 %collective-permute-start.30 = (bf16[128,1024]{1,0:T(8,128)(2,1)S(1)}, bf16[128,1024]{1,0:T(8,128)(2,1)S(1)}, u32[]{:S(2)}, u32[]{:S(2)}) collective-permute-start(bf16[128,1024]{1,0:T(8,128)(2,1)S(1)} %get-tuple-element.267), channel_id=1, source_target_pairs={{0,8},{8,16},{16,24},{24,28},{28,20},{20,12},{12,4},{4,0},{1,9},{9... | collective-permute-start | bytes 786440 | tf_op jit(solution)/shard_map/ppermute | solution.py:41
  201.7 23.8 %collective-permute-start.31 = (bf16[128,1024]{1,0:T(8,128)(2,1)S(1)}, bf16[128,1024]{1,0:T(8,128)(2,1)S(1)}, u32[]{:S(2)}, u32[]{:S(2)}) collective-permute-start(bf16[128,1024]{1,0:T(8,128)(2,1)S(1)} %get-tuple-element.268), channel_id=1, source_target_pairs={{0,4},{8,0},{16,8},{24,16},{28,24},{20,28},{12,20},{4,12},{1,5},{9... | collective-permute-start | bytes 786440 | tf_op jit(solution)/shard_map/ppermute | solution.py:41
  226.6 27.2 %collective-permute-start.32 = (bf16[256,1024]{1,0:T(8,128)(2,1)}, bf16[256,1024]{1,0:T(8,128)(2,1)}, u32[]{:S(2)}, u32[]{:S(2)}) collective-permute-start(bf16[256,1024]{1,0:T(8,128)(2,1)} %get-tuple-element.282), channel_id=1, source_target_pairs={{0,8},{8,16},{16,24},{24,28},{28,20},{20,12},{12,4},{4,0},{1,9},{9... | collective-permute-start | bytes 1572872 | tf_op jit(solution)/shard_map/ppermute | solution.py:41
  227.9 25.9 %collective-permute-start.33 = (bf16[256,1024]{1,0:T(8,128)(2,1)}, bf16[256,1024]{1,0:T(8,128)(2,1)}, u32[]{:S(2)}, u32[]{:S(2)}) collective-permute-start(bf16[256,1024]{1,0:T(8,128)(2,1)} %get-tuple-element.283), channel_id=1, source_target_pairs={{0,4},{8,0},{16,8},{24,16},{28,24},{20,28},{12,20},{4,12},{1,5},{9... | collective-permute-start | bytes 1572872 | tf_op jit(solution)/shard_map/ppermute | solution.py:41
  257.6 18.8 %collective-permute-start.34 = (bf16[256,1024]{1,0:T(8,128)(2,1)S(1)}, bf16[256,1024]{1,0:T(8,128)(2,1)S(1)}, u32[]{:S(2)}, u32[]{:S(2)}) collective-permute-start(bf16[256,1024]{1,0:T(8,128)(2,1)S(1)} %get-tuple-element.297), channel_id=1, source_target_pairs={{0,8},{8,16},{16,24},{24,28},{28,20},{20,12},{12,4},{4,0},{1,9},{9... | collective-permute-start | bytes 1572872 | tf_op jit(solution)/shard_map/ppermute | solution.py:41
  259.0 17.4 %collective-permute-start.35 = (bf16[256,1024]{1,0:T(8,128)(2,1)S(1)}, bf16[256,1024]{1,0:T(8,128)(2,1)S(1)}, u32[]{:S(2)}, u32[]{:S(2)}) collective-permute-start(bf16[256,1024]{1,0:T(8,128)(2,1)S(1)} %get-tuple-element.298), channel_id=1, source_target_pairs={{0,4},{8,0},{16,8},{24,16},{28,24},{20,28},{12,20},{4,12},{1,5},{9... | collective-permute-start | bytes 1572872 | tf_op jit(solution)/shard_map/ppermute | solution.py:41
  267.6 37.7 %collective-permute-start.42 = (bf16[704,1024]{1,0:T(8,128)(2,1)}, bf16[704,1024]{1,0:T(8,128)(2,1)S(1)}, u32[]{:S(2)}, u32[]{:S(2)}) collective-permute-start(bf16[704,1024]{1,0:T(8,128)(2,1)} %dynamic-slice_bitcast_fusion.2), channel_id=1, source_target_pairs={{0,1},{1,0},{2,3},{3,2},{4,5},{5,4},{6,7},{7,6},{8,9},{9,8},{10,11... | collective-permute-start | bytes 4325384 | tf_op jit(solution)/shard_map/ppermute | solution.py:177
  278.1 16.7 %collective-permute-start.39 = (bf16[128,1024]{1,0:T(8,128)(2,1)S(1)}, bf16[128,1024]{1,0:T(8,128)(2,1)S(1)}, u32[]{:S(2)}, u32[]{:S(2)}) collective-permute-start(bf16[128,1024]{1,0:T(8,128)(2,1)S(1)} %get-tuple-element.308), channel_id=1, source_target_pairs={{0,4},{8,0},{16,8},{24,16},{28,24},{20,28},{12,20},{4,12},{1,5},{9... | collective-permute-start | bytes 786440 | tf_op jit(solution)/shard_map/ppermute | solution.py:41
  283.1 14.3 %collective-permute-start.36 = (bf16[256,1024]{1,0:T(8,128)(2,1)S(1)}, bf16[256,1024]{1,0:T(8,128)(2,1)S(1)}, u32[]{:S(2)}, u32[]{:S(2)}) collective-permute-start(bf16[256,1024]{1,0:T(8,128)(2,1)S(1)} %get-tuple-element.304), channel_id=1, source_target_pairs={{0,8},{8,16},{16,24},{24,28},{28,20},{20,12},{12,4},{4,0},{1,9},{9... | collective-permute-start | bytes 1572872 | tf_op jit(solution)/shard_map/ppermute | solution.py:41
  286.2 26.0 %collective-permute-start.43 = (bf16[8,80,1024]{2,1,0:T(8,128)(2,1)}, bf16[8,80,1024]{2,1,0:T(8,128)(2,1)}, u32[]{:S(2)}, u32[]{:S(2)}) collective-permute-start(bf16[8,80,1024]{2,1,0:T(8,128)(2,1)} %dynamic-slice_bitcast_fusion.3), channel_id=1, source_target_pairs={{0,1},{1,0},{2,3},{3,2},{4,5},{5,4},{6,7},{7,6},{8,9},{9,8},{10,11... | collective-permute-start | bytes 3932168 | tf_op jit(solution)/shard_map/ppermute | solution.py:177
  296.2 26.1 %collective-permute-start.46 = (bf16[704,1024]{1,0:T(8,128)(2,1)S(1)}, bf16[704,1024]{1,0:T(8,128)(2,1)}, u32[]{:S(2)}, u32[]{:S(2)}) collective-permute-start(bf16[704,1024]{1,0:T(8,128)(2,1)S(1)} %dynamic-slice_bitcast_fusion.1), channel_id=1, source_target_pairs={{0,1},{1,0},{2,3},{3,2},{4,5},{5,4},{6,7},{7,6},{8,9},{9,8},{10,11... | collective-permute-start | bytes 4325384 | tf_op jit(solution)/shard_map/ppermute | solution.py:177
  307.0 31.4 %collective-permute-start.51 = (bf16[704,1024]{1,0:T(8,128)(2,1)}, bf16[704,1024]{1,0:T(8,128)(2,1)}, u32[]{:S(2)}, u32[]{:S(2)}) collective-permute-start(bf16[704,1024]{1,0:T(8,128)(2,1)} %fusion.3.kept), channel_id=1, source_target_pairs={{0,2},{1,3},{2,0},{3,1},{4,6},{5,7},{6,4},{7,5},{8,10},{9,11},{10,... | collective-permute-start | bytes 4325384 | tf_op jit(solution)/shard_map/ppermute | solution.py:177
  309.6 52.3 %collective-permute-start.52 = (bf16[704,1024]{1,0:T(8,128)(2,1)}, bf16[704,1024]{1,0:T(8,128)(2,1)}, u32[]{:S(2)}, u32[]{:S(2)}) collective-permute-start(bf16[704,1024]{1,0:T(8,128)(2,1)} %fusion.3.kept), channel_id=1, source_target_pairs={{0,1},{1,0},{2,3},{3,2},{4,5},{5,4},{6,7},{7,6},{8,9},{9,8},{10,11... | collective-permute-start | bytes 4325384 | tf_op jit(solution)/shard_map/ppermute | solution.py:177
  346.2 27.2 %collective-permute-start.56 = (bf16[704,1024]{1,0:T(8,128)(2,1)}, bf16[704,1024]{1,0:T(8,128)(2,1)}, u32[]{:S(2)}, u32[]{:S(2)}) collective-permute-start(bf16[704,1024]{1,0:T(8,128)(2,1)} %dynamic-slice_bitcast_fusion), channel_id=1, source_target_pairs={{0,1},{1,0},{2,3},{3,2},{4,5},{5,4},{6,7},{7,6},{8,9},{9,8},{10,11... | collective-permute-start | bytes 4325384 | tf_op jit(solution)/shard_map/ppermute | solution.py:177
  361.9 33.6 %collective-permute-start.61 = (bf16[704,1024]{1,0:T(8,128)(2,1)}, bf16[704,1024]{1,0:T(8,128)(2,1)}, u32[]{:S(2)}, u32[]{:S(2)}) collective-permute-start(bf16[704,1024]{1,0:T(8,128)(2,1)} %fusion.2.kept), channel_id=1, source_target_pairs={{0,2},{1,3},{2,0},{3,1},{4,6},{5,7},{6,4},{7,5},{8,10},{9,11},{10,... | collective-permute-start | bytes 4325384 | tf_op jit(solution)/shard_map/ppermute | solution.py:177
  376.4 48.2 %collective-permute-start.71 = (bf16[704,1024]{1,0:T(8,128)(2,1)}, bf16[704,1024]{1,0:T(8,128)(2,1)}, u32[]{:S(2)}, u32[]{:S(2)}) collective-permute-start(bf16[704,1024]{1,0:T(8,128)(2,1)} %fusion.1.kept), channel_id=1, source_target_pairs={{0,2},{1,3},{2,0},{3,1},{4,6},{5,7},{6,4},{7,5},{8,10},{9,11},{10,... | collective-permute-start | bytes 4325384 | tf_op jit(solution)/shard_map/ppermute | solution.py:177
  420.4 34.2 %collective-permute-start.78 = (bf16[704,1024]{1,0:T(8,128)(2,1)}, bf16[704,1024]{1,0:T(8,128)(2,1)}, u32[]{:S(2)}, u32[]{:S(2)}) collective-permute-start(bf16[704,1024]{1,0:T(8,128)(2,1)} %fusion.2.kept), channel_id=1, source_target_pairs={{0,1},{1,0},{2,3},{3,2},{4,5},{5,4},{6,7},{7,6},{8,9},{9,8},{10,11... | collective-permute-start | bytes 4325384 | tf_op jit(solution)/shard_map/ppermute | solution.py:177
  420.6 34.0 %collective-permute-start.79 = (bf16[704,1024]{1,0:T(8,128)(2,1)}, bf16[704,1024]{1,0:T(8,128)(2,1)}, u32[]{:S(2)}, u32[]{:S(2)}) collective-permute-start(bf16[704,1024]{1,0:T(8,128)(2,1)} %collective-permute-done.61.got), channel_id=1, source_target_pairs={{0,1},{1,0},{2,3},{3,2},{4,5},{5,4},{6,7},{7,6},{8,9},{9,8},{10,11... | collective-permute-start | bytes 4325384 | tf_op jit(solution)/shard_map/ppermute | solution.py:177
  424.6 15.5 %collective-permute-start.72 = (bf16[1,8,48,384]{3,2,1,0:T(8,128)(2,1)S(1)}, bf16[1,8,48,384]{3,2,1,0:T(8,128)(2,1)S(1)}, u32[]{:S(2)}, u32[]{:S(2)}) collective-permute-start(bf16[1,8,48,384]{3,2,1,0:T(8,128)(2,1)S(1)} %constant_dynamic-slice_fusion.1), channel_id=1, source_target_pairs={{0,2},{1,3},{2,0},{3,1},{4,6},{5,7},{6,4},{7,5},{8,10},{9,11},{10,... | collective-permute-start | bytes 884744 | tf_op jit(solution)/shard_map/ppermute | solution.py:177
  441.3 21.1 %all-to-all-start.1 = ((bf16[8,48,384]{2,1,0:T(8,128)(2,1)}), bf16[8,48,384]{2,1,0:T(8,128)(2,1)S(1)}, u32[]{:S(2)}, u32[]{:S(2)}) async-start(bf16[8,48,384]{2,1,0:T(8,128)(2,1)} %fusion.23), calls=%async_computation.1 | async-start | bytes 589824 | tf_op jit(solution)/shard_map/all_to_all | solution.py:1254
  454.6 24.6 %collective-permute-start.80 = (bf16[704,1024]{1,0:T(8,128)(2,1)}, bf16[704,1024]{1,0:T(8,128)(2,1)}, u32[]{:S(2)}, u32[]{:S(2)}) collective-permute-start(bf16[704,1024]{1,0:T(8,128)(2,1)} %fusion.1.kept), channel_id=1, source_target_pairs={{0,1},{1,0},{2,3},{3,2},{4,5},{5,4},{6,7},{7,6},{8,9},{9,8},{10,11... | collective-permute-start | bytes 4325384 | tf_op jit(solution)/shard_map/ppermute | solution.py:177
  459.4 19.8 %collective-permute-start.81 = (bf16[704,1024]{1,0:T(8,128)(2,1)}, bf16[704,1024]{1,0:T(8,128)(2,1)}, u32[]{:S(2)}, u32[]{:S(2)}) collective-permute-start(bf16[704,1024]{1,0:T(8,128)(2,1)} %collective-permute-done.71.got), channel_id=1, source_target_pairs={{0,1},{1,0},{2,3},{3,2},{4,5},{5,4},{6,7},{7,6},{8,9},{9,8},{10,11... | collective-permute-start | bytes 4325384 | tf_op jit(solution)/shard_map/ppermute | solution.py:177
  (186 other events, 1887.8 us)

commit v2 on v1

--- a/solution.py
+++ b/solution.py
@@ -1215,9 +1215,13 @@
     final.append(Sum([(grads_last, 0, span)], count))
     waits = (grads_last, sent(rings))
     rings = final
+    wider = None
     while not all(ring.done for ring in rings):
         step(rings, waits)
         waits = lasts(rings)
+        if wider is None:
+            wider = totals[1].finish()
+            waits = (waits, wider)
 
     mix_first, mix_last, final_first, final_last = (
         total_of(ring) for ring in (*sum_rings, *final)
@@ -1263,7 +1267,7 @@
 
     total_down, total_gate, total_up = (
         total.reshape(expert_count, unit_count, width)
-        for total in (wide, totals[1].finish(), totals[2].finish())
+        for total in (wide, wider, totals[2].finish())
     )
     return (
         block_out,

time: 494 us -> 503 us (1.018)
    ppermute x56, waiting for transfers between devices: 68.2 us -> 73.9 us  [ring_send(): return lax.ppermute(value, 'shard', pairs)]
    ppermute x26, starting transfers between devices: 45.1 us -> 50.2 us  [swap(): return lax.ppermute(value, axis, [(i, i ^ bit) for i in range(count)])]
    unnamed x280 -> x278, local copies, waits for them, and re-layouts: 61.5 us -> 61.5 us
  transfers between devices with their start and end apart: 84 -> 84, of which waited for: 27 -> 26; matrix products, arithmetic and copies ran while one was open for 17% -> 16% of each run, Pallas kernels for 30% -> 29%
where the time goes in v2:
time: 503 us; the launch traced here: 494 us
  Pallas kernels  159 us (32%)
  starting transfers between devices  105 us (21%)
  local copies, waits for them, and re-layouts  87.1 us (17%)
  waiting for transfers between devices  82.5 us (16%)
  matrix products  32.5 us (6%)
  other arithmetic  24.3 us (5%)
    pallas_call x6, Pallas kernels, experts(): pl.pallas_call(functools.partial(experts_kernel, static), out_shape=[low(...  82 us
    ppermute x56, waiting for transfers between devices, ring_send(): return lax.ppermute(value, 'shard', pairs)  73.9 us
    unnamed x278, local copies, waits for them, and re-layouts  61.5 us
    ppermute x26, starting transfers between devices, swap(): return lax.ppermute(value, axis, [(i, i ^ bit) for i in range(count)])  50.2 us
    ppermute x56, starting transfers between devices, ring_send(): return lax.ppermute(value, 'shard', pairs)  46.6 us
    dot_general x7, matrix products, dot_tn(): lax.dot_general(left, right, (((0,), (0,)), ((), ())), preferred_element_...  31.8 us
    pallas_call x4, Pallas kernels, attend_back(): pl.pallas_call(functools.partial(attend_back_kernel, seq, head, heads), o...  25.3 us
    pallas_call x2, Pallas kernels, attend(): pl.pallas_call(functools.partial(attend_kernel, seq, seqs, places, heads,...  15.7 us
  transfers between devices with their start and end apart: 84, of which 26 were waited for; matrix products, arithmetic and copies ran while one was open for 16% of the time, Pallas kernels for 29%

profile of v2, /device:TPU:1, one launch (start us, length us, event | category | flops | bytes accessed | tf_op | source)
XLA Modules:
  0.0 494.1 jit_solution(2910738941699085103)
XLA Ops:
  7.4 13.7 %collective-permute-done.refs_1_ = bf16[304,1024]{1,0:T(8,128)(2,1)S(1)} collective-permute-done((bf16[304,1024]{1,0:T(8,128)(2,1)S(1)}, bf16[304,1024]{1,0:T(8,128)(2,1)S(1)}, u32[]{:S(2)}, u32[]{:S(2)}) %collective-permute-start) | collective-permute-done | bytes 622624 | tf_op jit(solution)/shard_map/ppermute | solution.py:41
  26.3 4.6 all-to-all-start
  30.9 4.9 collective-permute-done.2.refs_3_
  41.7 7.8 %collective-permute-done.4.refs_5_ = bf16[304,1024]{1,0:T(8,128)(2,1)S(1)} collective-permute-done((bf16[304,1024]{1,0:T(8,128)(2,1)S(1)}, bf16[304,1024]{1,0:T(8,128)(2,1)S(1)}, u32[]{:S(2)}, u32[]{:S(2)}) %collective-permute-start.4) | collective-permute-done | bytes 622624 | tf_op jit(solution)/shard_map/ppermute | solution.py:41
  66.2 8.1 %attend.2 = (bf16[1024,1024]{1,0:T(8,128)(2,1)S(1)}, bf16[6,1024,64]{2,1,0:T(8,128)(2,1)S(1)}, bf16[256,1024]{1,0:T(8,128)(2,1)S(1)}, bf16[8,48,1024]{2,1,0:T(8,128)(2,1)S(1)}) custom-call(s32[19]{0:T(128)S(1)} %pad_add_fusion.meta, bf16[304,1024]{1,0:T(8,128)(2,1)S(1)} %concatenate.44.refs_0_, bf16[304,1024]{1,0:T(8,128)(2,1)S(1)} %copy-done.95, ...), custom_call_target="tpu_custom_call" | custom-call | flops 8000000000 | bytes 1000 | tf_op jit(solution)/shard_map/attend/pallas_call | solution.py:431
  78.8 7.6 %attend.3 = (bf16[1024,1024]{1,0:T(8,128)(2,1)S(1)}, bf16[6,1024,64]{2,1,0:T(8,128)(2,1)S(1)}, bf16[256,1024]{1,0:T(8,128)(2,1)S(1)}) custom-call(s32[19]{0:T(128)S(1)} %pad_add_fusion.meta, bf16[304,1024]{1,0:T(8,128)(2,1)S(1)} %concatenate.44.refs_0_, bf16[304,1024]{1,0:T(8,128)(2,1)S(1)} %copy-done.95, bf16[304,1024]{1,0:T(8,128)(2,1)S(1)} %copy-done.97, ...), custom_call_target="tpu_custom_call" | custom-call | flops 8000000000 | bytes 1000 | tf_op jit(solution)/shard_map/attend/pallas_call | solution.py:431
  95.2 8.5 %collective-permute-done.13.refs_4_ = bf16[256,1024]{1,0:T(8,128)(2,1)S(1)} collective-permute-done((bf16[256,1024]{1,0:T(8,128)(2,1)S(1)}, bf16[256,1024]{1,0:T(8,128)(2,1)S(1)}, u32[]{:S(2)}, u32[]{:S(2)}) %collective-permute-start.13) | collective-permute-done | bytes 524320 | tf_op jit(solution)/shard_map/ppermute | solution.py:41
  109.1 5.7 %collective-permute-done.15.refs_6_ = bf16[256,1024]{1,0:T(8,128)(2,1)S(1)} collective-permute-done((bf16[256,1024]{1,0:T(8,128)(2,1)S(1)}, bf16[256,1024]{1,0:T(8,128)(2,1)S(1)}, u32[]{:S(2)}, u32[]{:S(2)}) %collective-permute-start.15) | collective-permute-done | bytes 524320 | tf_op jit(solution)/shard_map/ppermute | solution.py:41
  135.1 10.6 %experts.6 = (bf16[2048,1024]{1,0:T(8,128)(2,1)}, bf16[2048,1024]{1,0:T(8,128)(2,1)}, bf16[2048,1024]{1,0:T(8,128)(2,1)}, bf16[2048,1408]{1,0:T(8,128)(2,1)}, bf...) custom-call(s32[19]{0:T(128)S(1)} %pad_add_fusion.meta, ...), custom_call_target="tpu_custom_call" | custom-call | flops 5502926848 | bytes 1000 | tf_op jit(solution)/shard_map/experts/pallas_call | solution.py:728
  147.3 10.8 %experts.7 = (bf16[2048,1024]{1,0:T(8,128)(2,1)}, bf16[2048,1024]{1,0:T(8,128)(2,1)}, bf16[2048,1024]{1,0:T(8,128)(2,1)}, bf16[2048,1408]{1,0:T(8,128)(2,1)}, bf...) custom-call(s32[19]{0:T(128)S(1)} %pad_add_fusion.meta, ...), custom_call_target="tpu_custom_call", output_to_operand_aliasing={{0}: (19, {}), {1}: (20, {}), {2}: (21, {}), {3}: (22, {}),... | custom-call | flops 5502926848 | bytes 1000 | tf_op jit(solution)/shard_map/experts/pallas_call | solution.py:728
  174.6 10.5 %experts.8 = (bf16[2048,1024]{1,0:T(8,128)(2,1)}, bf16[2048,1024]{1,0:T(8,128)(2,1)}, bf16[2048,1024]{1,0:T(8,128)(2,1)}, bf16[2048,1408]{1,0:T(8,128)(2,1)}, bf...) custom-call(s32[19]{0:T(128)S(1)} %pad_add_fusion.meta, ...), custom_call_target="tpu_custom_call", output_to_operand_aliasing={{0}: (19, {}), {1}: (20, {}), {2}: (21, {}), {3}: (22, {}),... | custom-call | flops 5502926848 | bytes 1000 | tf_op jit(solution)/shard_map/experts/pallas_call | solution.py:728
  188.7 10.6 %experts.9 = (bf16[2048,1024]{1,0:T(8,128)(2,1)}, bf16[2048,1024]{1,0:T(8,128)(2,1)}, bf16[2048,1024]{1,0:T(8,128)(2,1)}, bf16[2048,1408]{1,0:T(8,128)(2,1)}, bf...) custom-call(s32[19]{0:T(128)S(1)} %pad_add_fusion.meta, ...), custom_call_target="tpu_custom_call", output_to_operand_aliasing={{0}: (19, {}), {1}: (20, {}), {2}: (21, {}), {3}: (22, {}),... | custom-call | flops 5502926848 | bytes 1000 | tf_op jit(solution)/shard_map/experts/pallas_call | solution.py:728
  205.5 20.0 %experts.10 = (bf16[2048,1024]{1,0:T(8,128)(2,1)}, bf16[2048,1024]{1,0:T(8,128)(2,1)}, bf16[2048,1024]{1,0:T(8,128)(2,1)}, bf16[2048,1408]{1,0:T(8,128)(2,1)}, b...) custom-call(s32[19]{0:T(128)S(1)} %pad_add_fusion.meta, ...), custom_call_target="tpu_custom_call", output_to_operand_aliasing={{0}: (19, {}), {1}: (20, {}), {2}: (21, {}), {3}: (22, {}),... | custom-call | flops 11005853696 | bytes 1000 | tf_op jit(solution)/shard_map/experts/pallas_call | solution.py:728
  228.6 19.7 %experts.11 = (bf16[2048,1024]{1,0:T(8,128)(2,1)}, bf16[2048,1024]{1,0:T(8,128)(2,1)}, bf16[2048,1024]{1,0:T(8,128)(2,1)}, bf16[2048,1408]{1,0:T(8,128)(2,1)}, b...) custom-call(s32[19]{0:T(128)S(1)} %pad_add_fusion.meta, ...), custom_call_target="tpu_custom_call", output_to_operand_aliasing={{0}: (19, {}), {1}: (20, {}), {2}: (21, {}), {3}: (22, {}),... | custom-call | flops 11005853696 | bytes 1000 | tf_op jit(solution)/shard_map/experts/pallas_call | solution.py:728
  259.8 6.6 %convolution_convert_fusion.2 = bf16[1408,1024]{1,0:T(8,128)(2,1)S(1)} fusion(bf16[2048,1408]{1,0:T(8,128)(2,1)S(1)} %bitcast.204, bf16[2048,1024]{1,0:T(8,128)(2,1)S(1)} %copy-done.107), kind=kOutput, calls=%fused_computation.8 | convolution fusion | flops 5907021824 | bytes 12845056 | tf_op jit(solution)/shard_map/dot_general | solution.py:23
  267.7 8.8 %collective-permute-start.42 = (bf16[704,1024]{1,0:T(8,128)(2,1)}, bf16[704,1024]{1,0:T(8,128)(2,1)S(1)}, u32[]{:S(2)}, u32[]{:S(2)}) collective-permute-start(bf16[704,1024]{1,0:T(8,128)(2,1)} %dynamic-slice_bitcast_fusion.2), channel_id=1, source_target_pairs={{0,1},{1,0},{2,3},{3,2},{4,5},{5,4},{6,7},{7,6},{8,9},{9,8},{10,11... | collective-permute-start | bytes 4325384 | tf_op jit(solution)/shard_map/ppermute | solution.py:177
  278.2 4.8 convolution_convert_fusion.3
  288.3 6.4 %convolution_convert_fusion.1 = bf16[1408,1024]{1,0:T(8,128)(2,1)S(1)} fusion(bf16[2048,1408]{1,0:T(8,128)(2,1)S(1)} %bitcast.206, bf16[2048,1024]{1,0:T(8,128)(2,1)S(1)} %copy-done.106), kind=kOutput, calls=%fused_computation.7 | convolution fusion | flops 5907021824 | bytes 12845056 | tf_op jit(solution)/shard_map/dot_general | solution.py:23
  299.5 5.8 %attend_back.4 = (bf16[3,1024,64]{2,1,0:T(8,128)(2,1)S(1)}, f32[8,2048]{1,0:T(8,128)S(1)}) custom-call(s32[19]{0:T(128)S(1)} %pad_add_fusion.meta, bf16[6,1024,64]{2,1,0:T(8,128)(2,1)S(1)} %copy-done.103, bf16[6,1024,64]{2,1,0:T(8,128)(2,1)S(1)} %copy-done.103, bf16[6,1024,64]{2,1,0:T(8,128)(2,1)S(1)} %copy-done.103, bf16[8,256,1024]{2,1,0:T(8,128)(2,1)S(1)} %copy-done.4, ...), custom_call_target="tpu_custom_call" | custom-call | flops 6000000000 | bytes 1000 | tf_op jit(solution)/shard_map/attend_back/pallas_call | solution.py:845
  315.8 5.8 %attend_back.5 = (bf16[3,1024,64]{2,1,0:T(8,128)(2,1)S(1)}, f32[8,2048]{1,0:T(8,128)S(1)}) custom-call(s32[19]{0:T(128)S(1)} %pad_add_fusion.meta, bf16[6,1024,64]{2,1,0:T(8,128)(2,1)S(1)} %copy-done.103, bf16[6,1024,64]{2,1,0:T(8,128)(2,1)S(1)} %copy-done.103, bf16[6,1024,64]{2,1,0:T(8,128)(2,1)S(1)} %copy-done.103, bf16[8,256,1024]{2,1,0:T(8,128)(2,1)S(1)} %copy-done.4, ...), custom_call_target="tpu_custom_call" | custom-call | flops 6000000000 | bytes 1000 | tf_op jit(solution)/shard_map/attend_back/pallas_call | solution.py:845
  332.3 6.3 %collective-permute-done.51.got = bf16[704,1024]{1,0:T(8,128)(2,1)} collective-permute-done((bf16[704,1024]{1,0:T(8,128)(2,1)}, bf16[704,1024]{1,0:T(8,128)(2,1)}, u32[]{:S(2)}, u32[]{:S(2)}) %collective-permute-start.51) | collective-permute-done | bytes 1441824 | tf_op jit(solution)/shard_map/ppermute | solution.py:177
  338.6 6.4 %convolution_convert_fusion = bf16[1408,1024]{1,0:T(8,128)(2,1)S(1)} fusion(bf16[2048,1408]{1,0:T(8,128)(2,1)S(1)} %bitcast.208, bf16[2048,1024]{1,0:T(8,128)(2,1)S(1)} %copy-done.106), kind=kOutput, calls=%fused_computation.6 | convolution fusion | flops 5907021824 | bytes 12845056 | tf_op jit(solution)/shard_map/dot_general | solution.py:23
  346.3 5.4 %collective-permute-start.56 = (bf16[704,1024]{1,0:T(8,128)(2,1)}, bf16[704,1024]{1,0:T(8,128)(2,1)}, u32[]{:S(2)}, u32[]{:S(2)}) collective-permute-start(bf16[704,1024]{1,0:T(8,128)(2,1)} %dynamic-slice_bitcast_fusion), channel_id=1, source_target_pairs={{0,1},{1,0},{2,3},{3,2},{4,5},{5,4},{6,7},{7,6},{8,9},{9,8},{10,11... | collective-permute-start | bytes 4325384 | tf_op jit(solution)/shard_map/ppermute | solution.py:177
  352.7 6.2 %collective-permute-done.49.right = bf16[104,1024]{1,0:T(8,128)(2,1)S(1)} collective-permute-done((bf16[104,1024]{1,0:T(8,128)(2,1)S(1)}, bf16[104,1024]{1,0:T(8,128)(2,1)S(1)}, u32[]{:S(2)}, u32[]{:S(2)}) %collective-permute-start.49) | collective-permute-done | bytes 213024 | tf_op jit(solution)/shard_map/ppermute | solution.py:41
  372.4 4.9 widen.3
  384.4 6.9 %attend_back.6 = (bf16[3,1024,64]{2,1,0:T(8,128)(2,1)S(1)}, f32[8,2048]{1,0:T(8,128)S(1)}) custom-call(s32[19]{0:T(128)S(1)} %pad_add_fusion.meta, bf16[6,1024,64]{2,1,0:T(8,128)(2,1)S(1)} %copy-done.101, bf16[6,1024,64]{2,1,0:T(8,128)(2,1)S(1)} %copy-done.101, bf16[6,1024,64]{2,1,0:T(8,128)(2,1)S(1)} %copy-done.101, bf16[8,256,1024]{2,1,0:T(8,128)(2,1)S(1)} %copy-done.7, ...), custom_call_target="tpu_custom_call" | custom-call | flops 6000000000 | bytes 1000 | tf_op jit(solution)/shard_map/attend_back/pallas_call | solution.py:845
  393.9 6.8 %attend_back.7 = (bf16[3,1024,64]{2,1,0:T(8,128)(2,1)S(1)}, f32[8,2048]{1,0:T(8,128)S(1)}) custom-call(s32[19]{0:T(128)S(1)} %pad_add_fusion.meta, bf16[6,1024,64]{2,1,0:T(8,128)(2,1)S(1)} %copy-done.101, bf16[6,1024,64]{2,1,0:T(8,128)(2,1)S(1)} %copy-done.101, bf16[6,1024,64]{2,1,0:T(8,128)(2,1)S(1)} %copy-done.101, bf16[8,256,1024]{2,1,0:T(8,128)(2,1)S(1)} %copy-done.7, ...), custom_call_target="tpu_custom_call" | custom-call | flops 6000000000 | bytes 1000 | tf_op jit(solution)/shard_map/attend_back/pallas_call | solution.py:845
  419.2 4.2 collective-permute-start.72
  427.3 4.9 widen.4
  435.7 9.5 %collective-permute-done.59 = bf16[208,1024]{1,0:T(8,128)(2,1)S(1)} collective-permute-done((bf16[208,1024]{1,0:T(8,128)(2,1)S(1)}, bf16[208,1024]{1,0:T(8,128)(2,1)S(1)}, u32[]{:S(2)}, u32[]{:S(2)}) %collective-permute-start.59) | collective-permute-done | bytes 426016 | tf_op jit(solution)/shard_map/ppermute | solution.py:41
  453.0 4.1 all-to-all-start.1
  488.8 4.8 widen.5
  (576 shorter events, 239.7 us)
Async XLA Ops:
  5.2 15.8 %collective-permute-start = (bf16[304,1024]{1,0:T(8,128)(2,1)S(1)}, bf16[304,1024]{1,0:T(8,128)(2,1)S(1)}, u32[]{:S(2)}, u32[]{:S(2)}) collective-permute-start(bf16[304,1024]{1,0:T(8,128)(2,1)S(1)} %concatenate.44.refs_0_), channel_id=1, source_target_pairs={{0,8},{8,16},{16,24},{24,28},{28,20},{20,12},{12,4},{4,0},{1,9},{9... | collective-permute-start | bytes 1867784 | tf_op jit(solution)/shard_map/ppermute | solution.py:41
  7.4 14.6 %collective-permute-start.1 = (bf16[304,1024]{1,0:T(8,128)(2,1)S(1)}, bf16[304,1024]{1,0:T(8,128)(2,1)S(1)}, u32[]{:S(2)}, u32[]{:S(2)}) collective-permute-start(bf16[304,1024]{1,0:T(8,128)(2,1)S(1)} %concatenate.44.refs_0_), channel_id=1, source_target_pairs={{0,4},{8,0},{16,8},{24,16},{28,24},{20,28},{12,20},{4,12},{1,5},{9... | collective-permute-start | bytes 1867784 | tf_op jit(solution)/shard_map/ppermute | solution.py:41
  40.4 21.2 %collective-permute-start.8 = (bf16[8,32,384]{2,1,0:T(8,128)(2,1)S(1)}, bf16[8,32,384]{2,1,0:T(8,128)(2,1)S(1)}, u32[]{:S(2)}, u32[]{:S(2)}) collective-permute-start(bf16[8,32,384]{2,1,0:T(8,128)(2,1)S(1)} %all-to-all-done.refs_0_), channel_id=1, source_target_pairs={{0,2},{1,3},{2,0},{3,1},{4,6},{5,7},{6,4},{7,5},{8,10},{9,11},{10,... | collective-permute-start | bytes 589832 | tf_op jit(solution)/shard_map/ppermute | solution.py:177
  94.0 15.0 %collective-permute-start.19 = (bf16[8,32,1024]{2,1,0:T(8,128)(2,1)}, bf16[8,32,1024]{2,1,0:T(8,128)(2,1)}, u32[]{:S(2)}, u32[]{:S(2)}) collective-permute-start(bf16[8,32,1024]{2,1,0:T(8,128)(2,1)} %slice.201.refs_0_), channel_id=1, source_target_pairs={{0,2},{1,3},{2,0},{3,1},{4,6},{5,7},{6,4},{7,5},{8,10},{9,11},{10,... | collective-permute-start | bytes 1572872 | tf_op jit(solution)/shard_map/ppermute | solution.py:177
  105.3 17.2 %collective-permute-start.20 = (bf16[8,32,1024]{2,1,0:T(8,128)(2,1)}, bf16[8,32,1024]{2,1,0:T(8,128)(2,1)}, u32[]{:S(2)}, u32[]{:S(2)}) collective-permute-start(bf16[8,32,1024]{2,1,0:T(8,128)(2,1)} %slice.201.refs_0_), channel_id=1, source_target_pairs={{0,1},{1,0},{2,3},{3,2},{4,5},{5,4},{6,7},{7,6},{8,9},{9,8},{10,11... | collective-permute-start | bytes 1572872 | tf_op jit(solution)/shard_map/ppermute | solution.py:177
  120.4 25.3 %collective-permute-start.22 = (bf16[256,1024]{1,0:T(8,128)(2,1)}, bf16[256,1024]{1,0:T(8,128)(2,1)}, u32[]{:S(2)}, u32[]{:S(2)}) collective-permute-start(bf16[256,1024]{1,0:T(8,128)(2,1)} %copy-done.69), channel_id=1, source_target_pairs={{0,8},{8,16},{16,24},{24,28},{28,20},{20,12},{12,4},{4,0},{1,9},{9... | collective-permute-start | bytes 1572872 | tf_op jit(solution)/shard_map/ppermute | solution.py:41
  121.8 23.9 %collective-permute-start.23 = (bf16[256,1024]{1,0:T(8,128)(2,1)}, bf16[256,1024]{1,0:T(8,128)(2,1)}, u32[]{:S(2)}, u32[]{:S(2)}) collective-permute-start(bf16[256,1024]{1,0:T(8,128)(2,1)} %copy-done.69), channel_id=1, source_target_pairs={{0,4},{8,0},{16,8},{24,16},{28,24},{20,28},{12,20},{4,12},{1,5},{9... | collective-permute-start | bytes 1572872 | tf_op jit(solution)/shard_map/ppermute | solution.py:41
  158.0 27.1 %collective-permute-start.26 = (bf16[256,1024]{1,0:T(8,128)(2,1)}, bf16[256,1024]{1,0:T(8,128)(2,1)}, u32[]{:S(2)}, u32[]{:S(2)}) collective-permute-start(bf16[256,1024]{1,0:T(8,128)(2,1)} %collective-permute-done.24.refs_4_), channel_id=1, source_target_pairs={{0,8},{8,16},{16,24},{24,28},{28,20},{20,12},{12,4},{4,0},{1,9},{9... | collective-permute-start | bytes 1572872 | tf_op jit(solution)/shard_map/ppermute | solution.py:41
  159.5 25.7 %collective-permute-start.27 = (bf16[256,1024]{1,0:T(8,128)(2,1)}, bf16[256,1024]{1,0:T(8,128)(2,1)}, u32[]{:S(2)}, u32[]{:S(2)}) collective-permute-start(bf16[256,1024]{1,0:T(8,128)(2,1)} %collective-permute-done.25.refs_5_), channel_id=1, source_target_pairs={{0,4},{8,0},{16,8},{24,16},{28,24},{20,28},{12,20},{4,12},{1,5},{9... | collective-permute-start | bytes 1572872 | tf_op jit(solution)/shard_map/ppermute | solution.py:41
  200.4 25.1 %collective-permute-start.30 = (bf16[128,1024]{1,0:T(8,128)(2,1)S(1)}, bf16[128,1024]{1,0:T(8,128)(2,1)S(1)}, u32[]{:S(2)}, u32[]{:S(2)}) collective-permute-start(bf16[128,1024]{1,0:T(8,128)(2,1)S(1)} %get-tuple-element.267), channel_id=1, source_target_pairs={{0,8},{8,16},{16,24},{24,28},{28,20},{20,12},{12,4},{4,0},{1,9},{9... | collective-permute-start | bytes 786440 | tf_op jit(solution)/shard_map/ppermute | solution.py:41
  201.8 23.7 %collective-permute-start.31 = (bf16[128,1024]{1,0:T(8,128)(2,1)S(1)}, bf16[128,1024]{1,0:T(8,128)(2,1)S(1)}, u32[]{:S(2)}, u32[]{:S(2)}) collective-permute-start(bf16[128,1024]{1,0:T(8,128)(2,1)S(1)} %get-tuple-element.268), channel_id=1, source_target_pairs={{0,4},{8,0},{16,8},{24,16},{28,24},{20,28},{12,20},{4,12},{1,5},{9... | collective-permute-start | bytes 786440 | tf_op jit(solution)/shard_map/ppermute | solution.py:41
  226.6 27.2 %collective-permute-start.32 = (bf16[256,1024]{1,0:T(8,128)(2,1)}, bf16[256,1024]{1,0:T(8,128)(2,1)}, u32[]{:S(2)}, u32[]{:S(2)}) collective-permute-start(bf16[256,1024]{1,0:T(8,128)(2,1)} %get-tuple-element.282), channel_id=1, source_target_pairs={{0,8},{8,16},{16,24},{24,28},{28,20},{20,12},{12,4},{4,0},{1,9},{9... | collective-permute-start | bytes 1572872 | tf_op jit(solution)/shard_map/ppermute | solution.py:41
  228.0 25.8 %collective-permute-start.33 = (bf16[256,1024]{1,0:T(8,128)(2,1)}, bf16[256,1024]{1,0:T(8,128)(2,1)}, u32[]{:S(2)}, u32[]{:S(2)}) collective-permute-start(bf16[256,1024]{1,0:T(8,128)(2,1)} %get-tuple-element.283), channel_id=1, source_target_pairs={{0,4},{8,0},{16,8},{24,16},{28,24},{20,28},{12,20},{4,12},{1,5},{9... | collective-permute-start | bytes 1572872 | tf_op jit(solution)/shard_map/ppermute | solution.py:41
  257.6 18.8 %collective-permute-start.34 = (bf16[256,1024]{1,0:T(8,128)(2,1)S(1)}, bf16[256,1024]{1,0:T(8,128)(2,1)S(1)}, u32[]{:S(2)}, u32[]{:S(2)}) collective-permute-start(bf16[256,1024]{1,0:T(8,128)(2,1)S(1)} %get-tuple-element.297), channel_id=1, source_target_pairs={{0,8},{8,16},{16,24},{24,28},{28,20},{20,12},{12,4},{4,0},{1,9},{9... | collective-permute-start | bytes 1572872 | tf_op jit(solution)/shard_map/ppermute | solution.py:41
  259.1 17.4 %collective-permute-start.35 = (bf16[256,1024]{1,0:T(8,128)(2,1)S(1)}, bf16[256,1024]{1,0:T(8,128)(2,1)S(1)}, u32[]{:S(2)}, u32[]{:S(2)}) collective-permute-start(bf16[256,1024]{1,0:T(8,128)(2,1)S(1)} %get-tuple-element.298), channel_id=1, source_target_pairs={{0,4},{8,0},{16,8},{24,16},{28,24},{20,28},{12,20},{4,12},{1,5},{9... | collective-permute-start | bytes 1572872 | tf_op jit(solution)/shard_map/ppermute | solution.py:41
  267.7 37.7 %collective-permute-start.42 = (bf16[704,1024]{1,0:T(8,128)(2,1)}, bf16[704,1024]{1,0:T(8,128)(2,1)S(1)}, u32[]{:S(2)}, u32[]{:S(2)}) collective-permute-start(bf16[704,1024]{1,0:T(8,128)(2,1)} %dynamic-slice_bitcast_fusion.2), channel_id=1, source_target_pairs={{0,1},{1,0},{2,3},{3,2},{4,5},{5,4},{6,7},{7,6},{8,9},{9,8},{10,11... | collective-permute-start | bytes 4325384 | tf_op jit(solution)/shard_map/ppermute | solution.py:177
  278.1 16.7 %collective-permute-start.39 = (bf16[128,1024]{1,0:T(8,128)(2,1)S(1)}, bf16[128,1024]{1,0:T(8,128)(2,1)S(1)}, u32[]{:S(2)}, u32[]{:S(2)}) collective-permute-start(bf16[128,1024]{1,0:T(8,128)(2,1)S(1)} %get-tuple-element.308), channel_id=1, source_target_pairs={{0,4},{8,0},{16,8},{24,16},{28,24},{20,28},{12,20},{4,12},{1,5},{9... | collective-permute-start | bytes 786440 | tf_op jit(solution)/shard_map/ppermute | solution.py:41
  286.2 26.0 %collective-permute-start.43 = (bf16[8,80,1024]{2,1,0:T(8,128)(2,1)}, bf16[8,80,1024]{2,1,0:T(8,128)(2,1)}, u32[]{:S(2)}, u32[]{:S(2)}) collective-permute-start(bf16[8,80,1024]{2,1,0:T(8,128)(2,1)} %dynamic-slice_bitcast_fusion.3), channel_id=1, source_target_pairs={{0,1},{1,0},{2,3},{3,2},{4,5},{5,4},{6,7},{7,6},{8,9},{9,8},{10,11... | collective-permute-start | bytes 3932168 | tf_op jit(solution)/shard_map/ppermute | solution.py:177
  296.3 26.1 %collective-permute-start.46 = (bf16[704,1024]{1,0:T(8,128)(2,1)S(1)}, bf16[704,1024]{1,0:T(8,128)(2,1)}, u32[]{:S(2)}, u32[]{:S(2)}) collective-permute-start(bf16[704,1024]{1,0:T(8,128)(2,1)S(1)} %dynamic-slice_bitcast_fusion.1), channel_id=1, source_target_pairs={{0,1},{1,0},{2,3},{3,2},{4,5},{5,4},{6,7},{7,6},{8,9},{9,8},{10,11... | collective-permute-start | bytes 4325384 | tf_op jit(solution)/shard_map/ppermute | solution.py:177
  307.2 31.4 %collective-permute-start.51 = (bf16[704,1024]{1,0:T(8,128)(2,1)}, bf16[704,1024]{1,0:T(8,128)(2,1)}, u32[]{:S(2)}, u32[]{:S(2)}) collective-permute-start(bf16[704,1024]{1,0:T(8,128)(2,1)} %fusion.3.kept), channel_id=1, source_target_pairs={{0,2},{1,3},{2,0},{3,1},{4,6},{5,7},{6,4},{7,5},{8,10},{9,11},{10,... | collective-permute-start | bytes 4325384 | tf_op jit(solution)/shard_map/ppermute | solution.py:177
  309.6 56.7 %collective-permute-start.52 = (bf16[704,1024]{1,0:T(8,128)(2,1)}, bf16[704,1024]{1,0:T(8,128)(2,1)}, u32[]{:S(2)}, u32[]{:S(2)}) collective-permute-start(bf16[704,1024]{1,0:T(8,128)(2,1)} %fusion.3.kept), channel_id=1, source_target_pairs={{0,1},{1,0},{2,3},{3,2},{4,5},{5,4},{6,7},{7,6},{8,9},{9,8},{10,11... | collective-permute-start | bytes 4325384 | tf_op jit(solution)/shard_map/ppermute | solution.py:177
  325.6 43.8 %collective-permute-start.61 = (bf16[704,1024]{1,0:T(8,128)(2,1)}, bf16[704,1024]{1,0:T(8,128)(2,1)}, u32[]{:S(2)}, u32[]{:S(2)}) collective-permute-start(bf16[704,1024]{1,0:T(8,128)(2,1)} %fusion.2.kept), channel_id=1, source_target_pairs={{0,2},{1,3},{2,0},{3,1},{4,6},{5,7},{6,4},{7,5},{8,10},{9,11},{10,... | collective-permute-start | bytes 4325384 | tf_op jit(solution)/shard_map/ppermute | solution.py:177
  346.3 33.6 %collective-permute-start.56 = (bf16[704,1024]{1,0:T(8,128)(2,1)}, bf16[704,1024]{1,0:T(8,128)(2,1)}, u32[]{:S(2)}, u32[]{:S(2)}) collective-permute-start(bf16[704,1024]{1,0:T(8,128)(2,1)} %dynamic-slice_bitcast_fusion), channel_id=1, source_target_pairs={{0,1},{1,0},{2,3},{3,2},{4,5},{5,4},{6,7},{7,6},{8,9},{9,8},{10,11... | collective-permute-start | bytes 4325384 | tf_op jit(solution)/shard_map/ppermute | solution.py:177
  351.7 20.6 %collective-permute-start.53 = (bf16[704,1024]{1,0:T(8,128)(2,1)}, bf16[704,1024]{1,0:T(8,128)(2,1)}, u32[]{:S(2)}, u32[]{:S(2)}) collective-permute-start(bf16[704,1024]{1,0:T(8,128)(2,1)} %collective-permute-done.51.got), channel_id=1, source_target_pairs={{0,1},{1,0},{2,3},{3,2},{4,5},{5,4},{6,7},{7,6},{8,9},{9,8},{10,11... | collective-permute-start | bytes 4325384 | tf_op jit(solution)/shard_map/ppermute | solution.py:177
  369.5 57.8 %collective-permute-start.64 = (bf16[704,1024]{1,0:T(8,128)(2,1)}, bf16[704,1024]{1,0:T(8,128)(2,1)}, u32[]{:S(2)}, u32[]{:S(2)}) collective-permute-start(bf16[704,1024]{1,0:T(8,128)(2,1)} %fusion.2.kept), channel_id=1, source_target_pairs={{0,1},{1,0},{2,3},{3,2},{4,5},{5,4},{6,7},{7,6},{8,9},{9,8},{10,11... | collective-permute-start | bytes 4325384 | tf_op jit(solution)/shard_map/ppermute | solution.py:177
  372.4 54.9 %collective-permute-start.65 = (bf16[704,1024]{1,0:T(8,128)(2,1)}, bf16[704,1024]{1,0:T(8,128)(2,1)}, u32[]{:S(2)}, u32[]{:S(2)}) collective-permute-start(bf16[704,1024]{1,0:T(8,128)(2,1)} %collective-permute-done.61.got), channel_id=1, source_target_pairs={{0,1},{1,0},{2,3},{3,2},{4,5},{5,4},{6,7},{7,6},{8,9},{9,8},{10,11... | collective-permute-start | bytes 4325384 | tf_op jit(solution)/shard_map/ppermute | solution.py:177
  383.1 52.4 %collective-permute-start.73 = (bf16[704,1024]{1,0:T(8,128)(2,1)}, bf16[704,1024]{1,0:T(8,128)(2,1)}, u32[]{:S(2)}, u32[]{:S(2)}) collective-permute-start(bf16[704,1024]{1,0:T(8,128)(2,1)} %fusion.1.kept), channel_id=1, source_target_pairs={{0,2},{1,3},{2,0},{3,1},{4,6},{5,7},{6,4},{7,5},{8,10},{9,11},{10,... | collective-permute-start | bytes 4325384 | tf_op jit(solution)/shard_map/ppermute | solution.py:177
  419.2 16.0 %collective-permute-start.72 = (bf16[2,8,48,384]{3,2,1,0:T(8,128)(2,1)S(1)}, bf16[2,8,48,384]{3,2,1,0:T(8,128)(2,1)S(1)}, u32[]{:S(2)}, u32[]{:S(2)}) collective-permute-start(bf16[2,8,48,384]{3,2,1,0:T(8,128)(2,1)S(1)} %dynamic-slice_bitcast_fusion.4), channel_id=1, source_target_pairs={{0,1},{1,0},{2,3},{3,2},{4,5},{5,4},{6,7},{7,6},{8,9},{9,8},{10,11... | collective-permute-start | bytes 1769480 | tf_op jit(solution)/shard_map/ppermute | solution.py:177
  435.4 16.7 %collective-permute-start.74 = (bf16[1,8,48,384]{3,2,1,0:T(8,128)(2,1)S(1)}, bf16[1,8,48,384]{3,2,1,0:T(8,128)(2,1)S(1)}, u32[]{:S(2)}, u32[]{:S(2)}) collective-permute-start(bf16[1,8,48,384]{3,2,1,0:T(8,128)(2,1)S(1)} %constant_dynamic-slice_fusion.1), channel_id=1, source_target_pairs={{0,2},{1,3},{2,0},{3,1},{4,6},{5,7},{6,4},{7,5},{8,10},{9,11},{10,... | collective-permute-start | bytes 884744 | tf_op jit(solution)/shard_map/ppermute | solution.py:177
  453.0 19.1 %all-to-all-start.1 = ((bf16[8,48,384]{2,1,0:T(8,128)(2,1)}), bf16[8,48,384]{2,1,0:T(8,128)(2,1)S(1)}, u32[]{:S(2)}, u32[]{:S(2)}) async-start(bf16[8,48,384]{2,1,0:T(8,128)(2,1)} %fusion.23), calls=%async_computation.1 | async-start | bytes 589824 | tf_op jit(solution)/shard_map/all_to_all | solution.py:1258
  466.0 22.8 %collective-permute-start.80 = (bf16[704,1024]{1,0:T(8,128)(2,1)}, bf16[704,1024]{1,0:T(8,128)(2,1)}, u32[]{:S(2)}, u32[]{:S(2)}) collective-permute-start(bf16[704,1024]{1,0:T(8,128)(2,1)} %fusion.1.kept), channel_id=1, source_target_pairs={{0,1},{1,0},{2,3},{3,2},{4,5},{5,4},{6,7},{7,6},{8,9},{9,8},{10,11... | collective-permute-start | bytes 4325384 | tf_op jit(solution)/shard_map/ppermute | solution.py:177
  466.0 22.7 %collective-permute-start.81 = (bf16[704,1024]{1,0:T(8,128)(2,1)}, bf16[704,1024]{1,0:T(8,128)(2,1)}, u32[]{:S(2)}, u32[]{:S(2)}) collective-permute-start(bf16[704,1024]{1,0:T(8,128)(2,1)} %collective-permute-done.73.got), channel_id=1, source_target_pairs={{0,1},{1,0},{2,3},{3,2},{4,5},{5,4},{6,7},{7,6},{8,9},{9,8},{10,11... | collective-permute-start | bytes 4325384 | tf_op jit(solution)/shard_map/ppermute | solution.py:177
  (185 other events, 1679.0 us)
